TPU v7x, 256 devices: a whole 4x4x8 slice. The times are simulated.
256 devices in a mesh: dom: 64 (over z, x, core), blk: 4 (over y).
Axes of the slice: x: 4, y: 4, z: 8, core: 2. Of those that a mesh axis runs over, the one named last changes fastest.
Arguments:
- residual: float32 [4096, 135], P(('dom', 'blk')), may hold values from -112.5 to 112.5
- recycle_basis: float32 [8, 4096, 135], P(None, ('dom', 'blk')), may hold values from -5 to 5
- recycle_images: float32 [8, 4096, 135], P(None, ('dom', 'blk')), may hold values from -5 to 5
- jacobian: float32 [4096, 7, 135, 135], P(('dom', 'blk')), may hold values from -1.5 to 5.5
- neighbours: int32 [4096, 6], P(('dom', 'blk')), may hold values from -1 to 4095, as said below
- line_members: int32 [512, 8], replicated, may hold values from 0 to 4095, as said below
- line_pivots: float32 [512, 8, 135, 135], P(('dom', 'blk')), may hold values from -0.2 to 0.4
- line_lower: float32 [512, 7, 135, 135], P(('dom', 'blk')), may hold values from -0.375 to 0.375
- line_upper: float32 [512, 7, 135, 135], P(('dom', 'blk')), may hold values from -0.125 to 0.125
Outputs:
- correction: float32 [4096, 135], P(('dom', 'blk'))
- basis: float32 [9, 4096, 135], P(None, ('dom', 'blk'))
- hessenberg: float32 [9, 8], replicated
- residual_norm: float32 [], replicated
Inputs may be any that keep to these rules, and one draw needn't show every extreme that they name: `line_members`: each element lies in exactly one line. The lines of partition p (the 64 elements p * 64 to (p+1) * 64 - 1 on dom index p) are lines p * 8 onwards; they take exactly 8 elements from partition p-1, exactly 8 from partition p+1 (the first and last partition counting as beside each other) and all others from partition p. `neighbours`: every face neighbour lies in the element's own partition or in one of the two partitions beside it along dom, the first and last partition counting as beside each other.
All inputs are finite; a program needn't handle non-finite values.
Results may differ from a plain program's by a relative error of at most 0.0055.
Values sent between devices are 32-bit elements; how exact they have to be, the bound alone decides.
No kernel may reach another device: no remote copies, remote signals or barrier semaphores. Data moves between devices by JAX's collectives and lax.ppermute only.
A program may use at most 128 MiB of HBM per device.

v0:
```python
import functools

import jax
import jax.numpy as jnp
from jax import lax
from jax.experimental import pallas as pl
from jax.experimental.pallas import tpu as pltpu
from jax.sharding import PartitionSpec as P

STEPS = 8
EPS = 1e-06
KEPT = 2e-3
SAMPLE = 16
LANES = 128
ROWS = 136
INTERPRET = False
f32 = jnp.float32
bf16 = jnp.bfloat16
MIB = 1024 * 1024


def vmem_out(shape):
    if INTERPRET:
        return jax.ShapeDtypeStruct(shape, f32)
    return pltpu.VMEM(shape, f32)


def in_vmem(array):
    return array if INTERPRET else pltpu.with_memory_space_constraint(array, pltpu.VMEM)


def in_hbm(array):
    return array if INTERPRET else pltpu.with_memory_space_constraint(array, pltpu.HBM)


def call(body, out_shape, *args, scratch=(), limit=8, specs=None, after=None):
    spec = pl.BlockSpec(memory_space=pltpu.VMEM)
    specs = list(specs) if specs is not None else [spec] * len(args)
    inner, count = body, len(args)
    if after is not None:
        specs, args = specs + [pl.BlockSpec(memory_space=pl.ANY)], (*args, after)

        def body(*refs):
            inner(*refs[:count], *refs[count + 1 :])

    outs = out_shape if isinstance(out_shape, (list, tuple)) else None
    return pl.pallas_call(
        body,
        out_shape=out_shape,
        in_specs=specs,
        out_specs=[spec] * len(outs) if outs is not None else spec,
        scratch_shapes=list(scratch),
        compiler_params=pltpu.CompilerParams(vmem_limit_bytes=limit * MIB),
        interpret=INTERPRET,
    )(*args)


def pick(hits, pool):
    hits = hits.astype(bf16)
    high = pool.astype(bf16)
    rest = pool - high.astype(f32)
    mid = rest.astype(bf16)
    low = (rest - mid.astype(f32)).astype(bf16)
    dot = functools.partial(jnp.dot, preferred_element_type=f32)
    return dot(hits, high) + (dot(hits, mid) + dot(hits, low))


def halves(array):
    high = array.astype(bf16)
    return high, (array - high.astype(f32)).astype(bf16)


def product(left, right, dims):
    lh, ll = halves(left)
    rh, rl = halves(right)
    dot = lambda a, b: lax.dot_general(a, b, (dims, ((), ())), preferred_element_type=f32)
    return dot(lh, rh) + (dot(lh, rl) + dot(ll, rh))


def zero_body(*refs):
    refs[-1][...] = jnp.zeros(refs[-1].shape, f32)


def pack_body(jac_hbm, main_ref, rest_ref, token_ref):
    faces, rows, elems, cols = jac_hbm.shape
    chunk, group = 27, 9
    token_ref[...] = jnp.zeros(token_ref.shape, f32)
    extra = cols - LANES

    def step(block, at=None):
        at = (pl.program_id(0) if at is None else at) * chunk
        lane = lax.broadcasted_iota(jnp.int32, (elems, LANES), 1)

        def row(i):
            packed = jnp.zeros((elems, LANES), f32)
            for f in range(faces):
                main_ref[f, at + i] = block[f, i, :, 0:LANES]
                tail = jnp.concatenate(
                    [block[f, i, :, LANES:cols], jnp.zeros((elems, LANES - extra), f32)], 1
                )
                if f:
                    tail = pltpu.roll(tail, f * extra, 1)
                packed = packed + tail
            rest_ref[at + i] = packed

        def some(g, _):
            for n in range(group):
                row(g * group + n)
            return 0

        lax.fori_loop(0, chunk // group, some, 0)

    if INTERPRET:
        for c in range(rows // chunk):
            step(jac_hbm[:, c * chunk : (c + 1) * chunk], c)
        return
    pltpu.emit_pipeline(
        step,
        grid=(rows // chunk,),
        in_specs=[pl.BlockSpec((faces, chunk, elems, cols), lambda c: (0, c, 0, 0))],
    )(jac_hbm)


def invert_body(l, lines, pivot_ref, lower_ref, upper_ref, main_ref, rest_ref, token_ref, part_ref, wide_ref, side_ref):
    levels, height, _ = main_ref.shape
    cols = part_ref.shape[2]
    extra = cols - LANES
    rows_by_rows = ((1,), (1,))
    rows_by_cols = ((1,), (0,))
    pivot_rows = levels * cols
    token_ref[...] = jnp.zeros(token_ref.shape, f32)
    wide_ref[0:pivot_rows, :] = pivot_ref[l, :, 0:LANES]
    side_ref[0:pivot_rows, 0:extra] = pivot_ref[l, :, LANES:cols]

    def strided(first, count):
        at = pl.ds(first, cols, stride=count)
        return jnp.concatenate([wide_ref[at, :], side_ref[at, :][:, 0:extra]], 1)

    def paired(ref, k):
        wide_ref[pivot_rows:, :] = ref[k, :, 0:LANES]
        side_ref[pivot_rows:, 0:extra] = ref[k, :, LANES:cols]
        return strided(pivot_rows + l, lines)

    part_ref[...] = jnp.zeros(part_ref.shape, f32)
    part_ref[0, 0:cols, :] = strided(0, levels).T
    for k in range(1, levels):
        pivot = strided(k, levels)
        mixed = product(pivot, paired(lower_ref, k - 1), rows_by_cols)
        before = part_ref[k - 1, 0 : k * ROWS, :]
        part_ref[k, 0 : k * ROWS, :] = -product(before, mixed, rows_by_rows)
        part_ref[k, k * ROWS : k * ROWS + cols, :] = pivot.T

    def backward(i, _):
        k = levels - 2 - i
        part_ref[k] = part_ref[k] - product(part_ref[k + 1], paired(upper_ref, k), rows_by_rows)
        return 0

    lax.fori_loop(0, levels - 1, backward, 0)

    def emit(t, _):
        at = pl.ds(pl.multiple_of(t * ROWS, 8), ROWS)
        packed = jnp.zeros((ROWS, LANES), f32)
        for k in range(levels):
            main_ref[k, at, :] = part_ref[k, at, 0:LANES]
            tail = jnp.concatenate(
                [part_ref[k, at, LANES:cols], jnp.zeros((ROWS, LANES - extra), f32)], 1
            )
            packed = packed + (pltpu.roll(tail, k * extra, 1) if k else tail)
        rest_ref[at, :] = packed
        return 0

    lax.fori_loop(0, levels, emit, 0)


def solve_body(lines, *refs):
    blocks, refs = refs[: -4 - 2 * lines], refs[-4 - 2 * lines :]
    hits_ref, out_ref, pool_ref, wide_ref = refs[0], *refs[-3:]
    mains, rests = refs[1 : 1 + lines], refs[1 + lines : 1 + 2 * lines]
    levels = mains[0].shape[0]
    count = hits_ref.shape[0]
    cols = pool_ref.shape[1]
    extra = cols - LANES
    fill_pool(blocks, pool_ref)
    rhs = pick(hits_ref[...], pool_ref[...])
    rhs = jnp.concatenate([rhs, jnp.zeros((count, 2 * LANES - cols), f32)], 1)
    rhs = rhs.T[0:ROWS]
    for q in range(count):
        wide_ref[q] = jnp.broadcast_to(rhs[:, q : q + 1], (ROWS, LANES))
    for l in range(lines):

        def member(m, sums):
            sums = list(sums)
            for t in range(ROWS // 8):
                at = pl.ds(pl.multiple_of(m * ROWS + t * 8, 8), 8)
                value = wide_ref[l * levels + m, t * 8 : t * 8 + 8, :]
                for k in range(levels):
                    sums[k] = sums[k] + mains[l][k, at, :] * value
                sums[levels] = sums[levels] + rests[l][at, :] * value
            return tuple(sums)

        zero = jnp.zeros((8, LANES), f32)
        sums = lax.fori_loop(0, levels, member, (zero,) * (levels + 1))
        tails = jnp.sum(sums[levels], axis=0, keepdims=True)
        tails = jnp.broadcast_to(tails, (8, LANES))
        for k in range(levels):
            total = jnp.sum(sums[k], axis=0, keepdims=True)
            tail = pltpu.roll(tails, LANES - k * extra, 1) if k else tails
            at = slice(l * levels + k, l * levels + k + 1)
            out_ref[at, 0:LANES] = total
            out_ref[at, LANES:cols] = tail[0:1, 0:extra]


def fill_pool(blocks, pool_ref):
    at = 0
    for block in blocks:
        count = block.shape[0]
        pool_ref[at : at + count, :] = block[...]
        at += count


def operate(blocks, hits_ref, main_ref, rest_ref, pool_ref):
    faces, rows, elems, _ = main_ref.shape
    cols = pool_ref.shape[1]
    extra = cols - LANES
    fill_pool(blocks, pool_ref)
    field = pick(hits_ref[...], pool_ref[...])
    heads = [field[f * elems : (f + 1) * elems, 0:LANES] for f in range(faces)]
    packed = jnp.zeros((elems, LANES), f32)
    for f in range(faces):
        tail = jnp.concatenate(
            [field[f * elems : (f + 1) * elems, LANES:cols], jnp.zeros((elems, LANES - extra), f32)], 1
        )
        packed = packed + (pltpu.roll(tail, f * extra, 1) if f else tail)
    lane = lax.broadcasted_iota(jnp.int32, (elems, LANES), 1)

    def one(i):
        total = rest_ref[i] * packed
        for f in range(faces):
            total = total + main_ref[f, i] * heads[f]
        return jnp.sum(total, axis=1, keepdims=True)

    group = 16

    def some(g, image):
        for s in range(group):
            i = g * group + s
            image = jnp.where(lane == i, one(i), image)
        return image

    image = lax.fori_loop(0, LANES // group, some, jnp.zeros((elems, LANES), f32))
    tail = jnp.zeros((elems, LANES), f32)
    for c in range(extra):
        tail = jnp.where(lane == c, one(LANES + c), tail)
    return jnp.concatenate([image, tail[:, 0:extra]], 1)


def row_of(values):
    lane = lax.broadcasted_iota(jnp.int32, (1, LANES), 1)
    row = jnp.zeros((1, LANES), f32)
    for i, value in values.items():
        total = jnp.sum(jnp.sum(value, axis=0, keepdims=True), axis=1, keepdims=True)
        row = jnp.where(lane == i, total, row)
    return row


def lane_of(row, i):
    return row[:, i : i + 1]


UC, UU, CC = 13, 14, 15
SHIFT, SCALE, STEP = 0, 1, 2


def totals(parts_ref):
    return jnp.sum(parts_ref[...], axis=0, keepdims=True)


def project_body(images_in, residual_in, jac_in, pivot_in, out_ref, *refs):
    lines, levels = pivot_in.shape[0], pivot_in.shape[1] // jac_in.shape[1]
    sources = [
        images_in,
        residual_in,
        jac_in.at[0, 0:SAMPLE],
        pivot_in.at[:, 0 : SAMPLE * levels, :],
    ]
    if INTERPRET:
        refs = [source[...] for source in sources]
    else:
        *refs, sems = refs
        copies = [
            pltpu.make_async_copy(source, ref, sems.at[n])
            for n, (source, ref) in enumerate(zip(sources, refs))
        ]
        for copy in copies:
            copy.start()
        for copy in copies:
            copy.wait()
    images_ref, residual_ref, jac_ref, pivot_ref = refs
    residual = residual_ref[...]
    products = {k: images_ref[k] * residual for k in range(STEPS)}
    lane = lax.broadcasted_iota(jnp.int32, jac_ref.shape[1:], 1)
    own = jnp.zeros(jac_ref.shape[1:], f32)
    for i in range(SAMPLE):
        own = jnp.where(lane == i, jac_ref[i], own)
    products[STEPS] = own
    shape = (levels, pivot_ref.shape[2])
    lane = lax.broadcasted_iota(jnp.int32, shape, 1)
    own = jnp.zeros(shape, f32)
    for l in range(lines):
        for i in range(SAMPLE):
            own = own + jnp.where(lane == i, pivot_ref[l, i * levels : (i + 1) * levels], 0.0)
    products[STEPS + 1] = own
    out_ref[...] = row_of(products)


def deflate_body(entries, parts_ref, residual_ref, basis_ref, images_ref, correction_ref, start_ref):
    row = totals(parts_ref) / entries
    correction = jnp.zeros(residual_ref.shape, f32)
    start = residual_ref[...]
    for k in range(basis_ref.shape[0]):
        weight = lane_of(row, k)
        correction = correction + weight * basis_ref[k]
        start = start - weight * images_ref[k]
    correction_ref[...] = correction
    start_ref[...] = start


def shift_of(row, count):
    return lane_of(row, STEPS) / count * (lane_of(row, STEPS + 1) / count)


def power_body(count, *refs):
    *blocks, u_ref, row_ref, hits_ref, main_ref, rest_ref, out_ref, pool_ref = refs
    image = operate(blocks, hits_ref, main_ref, rest_ref, pool_ref)
    out_ref[...] = image - shift_of(row_ref[...], count) * u_ref[...]


def power_last_body(count, *refs):
    blocks, vectors, refs = refs[: -8 - STEPS], refs[-8 - STEPS : -8], refs[-8:]
    u_ref, row_ref, hits_ref, main_ref, rest_ref, out_ref, part_ref, pool_ref = refs
    image = operate(blocks, hits_ref, main_ref, rest_ref, pool_ref)
    last = image - shift_of(row_ref[...], count) * u_ref[...]
    out_ref[...] = last
    vectors = [v[...] for v in vectors] + [last]
    at = lax.broadcasted_iota(jnp.int32, part_ref.shape, 0)
    lane = lax.broadcasted_iota(jnp.int32, part_ref.shape, 1)
    part = jnp.zeros(part_ref.shape, f32)
    for k, right in enumerate(vectors):
        for i in range(k + 1):
            total = jnp.sum(vectors[i] * right, axis=0, keepdims=True)
            total = jnp.sum(total, axis=1, keepdims=True)
            here = ((at == i) & (lane == k)) | ((at == k) & (lane == i))
            part = jnp.where(here, total, part)
    part_ref[...] = part


def combine_body(entries, count, *refs):
    gram_ref, row_ref, *vectors = refs[: 3 + STEPS]
    basis_out, hess_out, norm_ref, sure_ref = refs[3 + STEPS :]
    shift = shift_of(row_ref[...], count)
    gram = gram_ref[...] / entries
    size = jnp.abs(gram)
    at = lax.broadcasted_iota(jnp.int32, gram.shape, 0)
    lane = lax.broadcasted_iota(jnp.int32, gram.shape, 1)

    def across(values):
        return jnp.sum(values, axis=1, keepdims=True)

    def turned(column):
        return jnp.sum(jnp.where(at == lane, column, 0.0), axis=0, keepdims=True)

    def times(matrix, row):
        return turned(across(matrix * row))

    first = lane[0:1]
    norm = jnp.sqrt(gram[0:1, 0:1] + EPS)
    norm_ref[...] = jnp.broadcast_to(norm, (1, LANES))
    newest = jnp.where(first == 0, 1.0 / norm, 0.0)
    known = jnp.where(at == 0, newest, 0.0)
    sure = jnp.full((1, 1), 1.0, f32)
    for j in range(STEPS):
        moved = pltpu.roll(jnp.broadcast_to(newest, (8, LANES)), 1, 1)[0:1]
        image = moved + shift * newest
        inner = across(known * times(gram, image))
        reduced = image - jnp.sum(known * inner, axis=0, keepdims=True)
        square = across(reduced * times(gram, reduced))
        terms = across(jnp.abs(reduced) * times(size, jnp.abs(reduced)))
        sure = jnp.where(square > KEPT * terms, sure, 0.0)
        below = jnp.sqrt(jnp.maximum(square, 0.0) + EPS)
        column = jnp.where(first <= j, turned(inner), 0.0)
        hess_out[j : j + 1, :] = jnp.where(first == j + 1, below, column)
        newest = reduced / below
        known = jnp.where(at == j + 1, newest, known)
    sure_ref[...] = jnp.broadcast_to(sure, (1, LANES))
    vectors = [v[...] for v in vectors]
    for j in range(STEPS + 1):
        value = known[j : j + 1, 0:1] * vectors[0]
        for k in range(1, j + 1):
            value = value + known[j : j + 1, k : k + 1] * vectors[k]
        basis_out[j] = value


def first_body(*refs):
    *blocks, u_ref, hits_ref, main_ref, rest_ref, c_ref, part_ref, pool_ref = refs
    c = operate(blocks, hits_ref, main_ref, rest_ref, pool_ref)
    c_ref[...] = c
    u = u_ref[...]
    part_ref[...] = row_of({UC: u * c, UU: u * u, CC: c * c})


def advance(entries, row, u, c, known, basis):
    scale, step = lane_of(known, SCALE), lane_of(known, STEP)
    norm = jnp.sqrt(lane_of(row, UU) / entries + EPS / (scale * scale))
    inverse = 1.0 / norm
    here = u * inverse
    image = c * inverse
    lane = lax.broadcasted_iota(jnp.int32, (1, LANES), 1)
    own = lane_of(row, UC) * inverse * inverse / entries
    column = jnp.where(lane < STEPS, row * inverse / entries, 0.0)
    column = jnp.where(lane.astype(f32) == step, own, column)
    scale_next = jnp.sqrt(lane_of(row, CC) * inverse * inverse / entries + EPS)
    reduced = image - own * here
    for i in range(STEPS):
        reduced = reduced - lane_of(row, i) * inverse / entries * basis[i]
    return here, image, inverse, own, column, scale * norm, reduced / scale_next, scale_next


def place(out_ref, in_ref, step, value):
    for i in range(in_ref.shape[0]):
        out_ref[i] = jnp.where(step == i, value, in_ref[i])


def record(hess_out, hess_ref, step, column, below):
    at = lax.broadcasted_iota(jnp.int32, hess_ref.shape, 0).astype(f32)
    lane = lax.broadcasted_iota(jnp.int32, hess_ref.shape, 1).astype(f32)
    hess = jnp.where(at == step, column, hess_ref[...])
    hess_out[...] = jnp.where((at == STEPS) & (lane == step), below, hess)


def numbers(shift, scale, step):
    lane = lax.broadcasted_iota(jnp.int32, (1, LANES), 1)
    row = jnp.where(lane == SHIFT, shift, jnp.zeros((1, LANES), f32))
    row = jnp.where(lane == SCALE, scale, row)
    return jnp.where(lane == STEP, step, row)


def next_body(entries, *refs):
    *blocks, hits_ref, main_ref, rest_ref, sums_ref, u_ref, c_ref, known_ref = refs[:-12]
    basis_ref, images_ref, hess_ref, basis_out, images_out, hess_out = refs[-12:-6]
    u_out, c_out, v_out, known_out, part_ref, pool_ref = refs[-6:]
    w = operate(blocks, hits_ref, main_ref, rest_ref, pool_ref)
    known = known_ref[...]
    step = lane_of(known, STEP)
    row = totals(sums_ref)
    here, image, inverse, own, column, below, u, scale = advance(
        entries, row, u_ref[...], c_ref[...], known, basis_ref
    )
    moved = w * inverse - (own - lane_of(known, SHIFT)) * image
    for i in range(STEPS):
        moved = moved - lane_of(row, i) * inverse / entries * images_ref[i]
    c = moved / scale
    place(basis_out, basis_ref, step, here)
    place(images_out, images_ref, step, image)
    record(hess_out, hess_ref, step, column, below)
    u_out[...] = u
    c_out[...] = c
    v_out[...] = c - own * u
    known_out[...] = numbers(own, scale, step + 1.0)
    products = {i: jnp.where(step == i, here, basis_ref[i]) * c for i in range(STEPS)}
    products.update({UC: u * c, UU: u * u, CC: c * c})
    part_ref[...] = row_of(products)


def last_body(entries, sums_ref, u_ref, c_ref, known_ref, basis_ref, hess_ref, *outs):
    basis_out, hess_out, u_out, known_out, part_ref = outs
    known = known_ref[...]
    step = lane_of(known, STEP)
    here, _, _, own, column, below, u, scale = advance(
        entries, totals(sums_ref), u_ref[...], c_ref[...], known, basis_ref
    )
    place(basis_out, basis_ref, step, here)
    record(hess_out, hess_ref, step, column, below)
    u_out[...] = u
    known_out[...] = numbers(own, scale, step + 1.0)
    part_ref[...] = row_of({UU: u * u})


def finish_body(entries, sums_ref, u_ref, known_ref, basis_ref, hess_ref, basis_out, hess_out, norm_ref):
    scale = lane_of(known_ref[...], SCALE)
    norm = jnp.sqrt(lane_of(totals(sums_ref), UU) / entries + EPS / (scale * scale))
    for i in range(STEPS):
        basis_out[i] = basis_ref[i]
    basis_out[STEPS] = u_ref[...] / norm
    lane = lax.broadcasted_iota(jnp.int32, (1, LANES), 1)
    norms = hess_ref[STEPS : STEPS + 1, :]
    for j in range(STEPS):
        below = lane_of(norms, j + 1) if j + 1 < STEPS else scale * norm
        hess_out[j : j + 1, :] = jnp.where(lane == j + 1, below, hess_ref[j : j + 1, :])
    norm_ref[...] = norms


def shifted(array, d_dom, d_blk):
    doms, blks = lax.axis_size("dom"), lax.axis_size("blk")
    if d_dom == 0 and d_blk == 0:
        return array
    pairs = []
    for d in range(doms):
        for b in range(blks):
            source = ((d + d_dom) % doms) * blks + (b + d_blk) % blks
            pairs.append((source, d * blks + b))
    return lax.ppermute(array, ("dom", "blk"), pairs)


def around(array, reach):
    blks = lax.axis_size("blk")
    whole = jnp.concatenate([shifted(array, 0, b) for b in range(blks)], 0)
    return [shifted(whole, d, 0) for d in range(-reach, reach + 1)]


def added(part, beside=()):
    beside = list(beside)
    doms, blks = lax.axis_size("dom"), lax.axis_size("blk")
    devices = doms * blks
    reach = 1
    while reach < devices:
        ways = 4 if reach * 4 <= devices else 2
        others = [
            lax.ppermute(part, ("dom", "blk"), [(n ^ (k * reach), n) for n in range(devices)])
            for k in range(1, ways)
        ]
        work = beside.pop(0) if beside else None
        zeros = work(part) if work is not None else None
        if ways == 4:
            part = (part + others[0]) + (others[1] + others[2])
        else:
            part = part + others[0]
        if zeros is not None:
            part = part + zeros
        reach *= ways
    for work in beside:
        part = part + work(part)
    return part


def matrices_of(jacobian, line_pivots, line_lower, line_upper):
    elems, faces, cols, _ = jacobian.shape
    lines, levels = line_pivots.shape[:2]
    height = levels * ROWS
    token = jax.ShapeDtypeStruct((1, LANES), f32)
    kept = {}

    def pack(after=None):
        main, rest, done = call(
            pack_body,
            [vmem_out((faces, cols, elems, LANES)), vmem_out((cols, elems, LANES)), token],
            in_hbm(jnp.transpose(jacobian, (1, 2, 0, 3))),
            specs=[pl.BlockSpec(memory_space=pltpu.VMEM if INTERPRET else pltpu.HBM)],
            limit=8,
            after=after,
        )
        kept["jac"] = in_vmem(main), in_vmem(rest)
        return done

    pivots = jnp.transpose(line_pivots, (0, 2, 1, 3)).reshape(lines, cols * levels, cols)
    lower = jnp.transpose(line_lower, (1, 2, 0, 3)).reshape(levels - 1, cols * lines, cols)
    upper = jnp.transpose(line_upper, (1, 2, 0, 3)).reshape(levels - 1, cols * lines, cols)

    def invert(l, after=None):
        main, rest, done = call(
            functools.partial(invert_body, l, lines),
            [vmem_out((levels, height, LANES)), vmem_out((height, LANES)), token],
            pivots,
            lower,
            upper,
            scratch=[
                pltpu.VMEM((levels, height, cols), f32),
                pltpu.VMEM(((levels + lines) * cols, LANES), f32),
                pltpu.VMEM(((levels + lines) * cols, LANES), f32),
            ],
            limit=20,
            after=after,
        )
        kept[l] = in_vmem(main), in_vmem(rest)
        return done

    def lay_out(_):
        anywhere = pl.BlockSpec(memory_space=pl.ANY)
        return call(zero_body, token, lower, upper, specs=[anywhere] * 2)

    return lay_out, invert, pack, kept


def per_device(residual, recycle_basis, recycle_images, jacobian, neighbours, line_members,
               line_pivots, line_lower, line_upper):
    elems, cols = residual.shape
    doms, blks = lax.axis_size("dom"), lax.axis_size("blk")
    lines, levels = line_pivots.shape[:2]
    entries = float(elems * cols * doms * blks)
    count = float(elems * SAMPLE * doms * blks)
    dom, blk = lax.axis_index("dom"), lax.axis_index("blk")
    devices = doms * blks
    row = jax.ShapeDtypeStruct((1, LANES), f32)
    rows = jax.ShapeDtypeStruct((elems, cols), f32)

    members = line_members.reshape(devices, elems)
    near = jnp.array([(d, b) for d in range(-2, 3) for b in range(blks)], jnp.int32)
    at = (dom + near[:, 0] + doms) % doms * blks + (blk + near[:, 1]) % blks
    line_ids = members[at].reshape(-1)
    near_own = at[blks : 4 * blks]
    elem_ids = (near_own[:, None] * elems + jnp.arange(elems, dtype=jnp.int32)).reshape(-1)
    me = dom * blks + blk
    own_ids = me * elems + jnp.arange(elems, dtype=jnp.int32)
    wanted = jnp.concatenate([own_ids[None], neighbours.T], 0).reshape(-1)
    stencil = (wanted[:, None] == line_ids[None, :]).astype(f32)
    mine = lax.dynamic_slice_in_dim(members, me, 1, 0)[0]
    entering = (mine[:, None] == elem_ids[None, :]).astype(f32)
    stencil_pool = pltpu.VMEM((stencil.shape[1], cols), f32)

    jac = jnp.transpose(jacobian, (1, 2, 0, 3))
    pivots = jnp.transpose(line_pivots, (0, 2, 1, 3)).reshape(lines, cols * levels, cols)
    wide = SAMPLE * levels
    part = call(
        project_body,
        row,
        *map(in_hbm, (recycle_images, residual, jac, pivots)),
        specs=[pl.BlockSpec(memory_space=pltpu.VMEM if INTERPRET else pltpu.HBM)] * 4,
        scratch=[]
        if INTERPRET
        else [
            pltpu.VMEM(recycle_images.shape, f32),
            pltpu.VMEM(residual.shape, f32),
            pltpu.VMEM((SAMPLE, elems, cols), f32),
            pltpu.VMEM((lines, wide, cols), f32),
            pltpu.SemaphoreType.DMA((4,)),
        ],
    )
    lay_out, invert, pack, kept = matrices_of(jacobian, line_pivots, line_lower, line_upper)
    inverts = [functools.partial(invert, l) for l in range(lines)]
    projected = added(part, [lay_out, None, *inverts])
    correction, start = call(
        functools.partial(deflate_body, entries),
        [rows, rows],
        projected,
        residual,
        recycle_basis,
        recycle_images,
    )

    pack(start)

    def precondition(v, kept):
        z = call(
            functools.partial(solve_body, lines),
            rows,
            *around(v, 1),
            entering,
            *[kept[l][0] for l in range(lines)],
            *[kept[l][1] for l in range(lines)],
            scratch=[
                pltpu.VMEM((entering.shape[1], cols), f32),
                pltpu.VMEM((elems, ROWS, LANES), f32),
            ],
        )
        return around(z, 2)

    vectors = [start]
    matrix = jax.ShapeDtypeStruct((2 * STEPS, LANES), f32)
    for j in range(STEPS):
        last = j == STEPS - 1
        pool = precondition(vectors[-1], kept)
        result = call(
            functools.partial(power_last_body if last else power_body, count),
            [rows, matrix] if last else rows,
            *pool,
            *(vectors if last else ()),
            vectors[-1],
            projected,
            stencil,
            *kept["jac"],
            scratch=[stencil_pool],
        )
        vectors.append(result[0] if last else result)
    gram = added(result[1])
    small = jax.ShapeDtypeStruct((STEPS, LANES), f32)
    stacked = jax.ShapeDtypeStruct((STEPS + 1, elems, cols), f32)
    basis, hessenberg, norm, sure = call(
        functools.partial(combine_body, entries, count),
        [stacked, small, row, row],
        gram,
        projected,
        *vectors,
    )

    def stepwise(start):
        _, invert, pack, kept = matrices_of(jacobian, line_pivots, line_lower, line_upper)
        for l in range(lines):
            invert(l)
        pack()
        matrices = (stencil, *kept["jac"])
        c, part = call(
            first_body,
            [rows, row],
            *precondition(start, kept),
            start,
            *matrices,
            scratch=[stencil_pool],
        )
        stack = jax.ShapeDtypeStruct((STEPS, elems, cols), f32)

        def step(_, state):
            basis, images, hessenberg, u, c, v, known, part = state
            return tuple(
                call(
                    functools.partial(next_body, entries),
                    [stack, stack, matrix, rows, rows, rows, row, row],
                    *precondition(v, kept),
                    *matrices,
                    added(part),
                    u,
                    c,
                    known,
                    basis,
                    images,
                    hessenberg,
                    scratch=[stencil_pool],
                )
            )

        empty = jnp.zeros(stack.shape, f32)
        known = jnp.zeros((1, LANES), f32).at[0, SCALE].set(1.0)
        state = (empty, empty, jnp.zeros(matrix.shape, f32), start, c, c, known, part)
        basis, _, hessenberg, u, c, _, known, part = lax.fori_loop(0, STEPS - 1, step, state)
        basis, hessenberg, u, known, part = call(
            functools.partial(last_body, entries),
            [stack, matrix, rows, row, row],
            added(part),
            u,
            c,
            known,
            basis,
            hessenberg,
        )
        return tuple(
            call(
                functools.partial(finish_body, entries),
                [stacked, small, row],
                added(part),
                u,
                known,
                basis,
                hessenberg,
            )
        )

    basis, hessenberg, norm = lax.cond(
        sure[0, 0] > 0.5, lambda start: (basis, hessenberg, norm), stepwise, start
    )
    return correction, basis, hessenberg[:, : STEPS + 1].T, norm[0, 0]


def solution(mesh):
    both = ("dom", "blk")
    in_specs = (
        P(both, None),
        P(None, both, None),
        P(None, both, None),
        P(both, None, None, None),
        P(both, None),
        P(),
        P(both, None, None, None),
        P(both, None, None, None),
        P(both, None, None, None),
    )
    out_specs = (P(both, None), P(None, both, None), P(), P())
    return jax.shard_map(
        per_device, mesh=mesh, in_specs=in_specs, out_specs=out_specs, check_vma=False
    )
```

profile of v0, /device:TPU:68, one launch (start us, length us, event | category | flops | bytes accessed | tf_op | source)
XLA Modules:
  0.0 373.1 jit_solution(10066419229600800543)
XLA Ops:
  2.0 3.1 collective-permute-start.62
  6.7 2.6 reshape.103.refs_1_.refs_2_
  9.3 3.5 reshape.102.refs_0_.refs_1_
  18.2 2.1 collective-permute-start.68
  20.4 3.1 collective-permute-start.66
  23.6 11.8 %shard_map.131 = (f32[8,1088,128]{2,1,0:T(8,128)S(1)}, f32[1088,128]{1,0:T(8,128)S(1)}, f32[1,128]{1,0:T(1,128)S(1)}) custom-call(f32[2,1080,135]{2,1,0:T(8,128)} %bitcast.50, f32[7,270,135]{2,1,0:T(8,128)S(1)} %copy-done.11, f32[7,270,135]{2,1,0:T(8,128)S(1)} %reshape.103.refs_1_.refs_2_, f32[1,128]{1,0:T(1,128)S(1)} %add_add_fusion.19.refs_3_), custom_call_target="tpu_custom_call" | custom-call | tf_op jit(solution)/shard_map/pallas_call | solution.py:47
  35.4 2.0 copy-done
  37.5 4.6 %collective-permute-start.71 = (f32[1,128]{1,0:T(1,128)S(1)}, f32[1,128]{1,0:T(1,128)S(1)}, u32[]{:S(2)}, u32[]{:S(2)}) collective-permute-start(f32[1,128]{1,0:T(1,128)S(1)} %add_add_fusion.18.refs_3_), channel_id=1, source_target_pairs={{192,0},{193,1},{194,2},{195,3},{196,4},{197,5},{198,6},{199,7},{2... | collective-permute-start | bytes 1544 | tf_op jit(solution)/shard_map/ppermute | solution.py:528
  46.0 12.0 %shard_map.132 = (f32[8,1088,128]{2,1,0:T(8,128)S(1)}, f32[1088,128]{1,0:T(8,128)S(1)}, f32[1,128]{1,0:T(1,128)S(1)}) custom-call(f32[2,1080,135]{2,1,0:T(8,128)} %bitcast.51, f32[7,270,135]{2,1,0:T(8,128)S(1)} %copy-done.12, f32[7,270,135]{2,1,0:T(8,128)S(1)} %reshape.103.refs_1_.refs_2_, f32[1,128]{1,0:T(1,128)S(1)} %add_add_fusion.18.refs_3_), custom_call_target="tpu_custom_call" | custom-call | tf_op jit(solution)/shard_map/pallas_call | solution.py:47
  60.6 2.9 collective-permute-start.73
  64.9 2.4 collective-permute-done.72
  69.9 1.9 collective-permute-done.75.refs_0_
  73.6 3.9 %collective-permute-start.78 = (f32[16,135]{1,0:T(8,128)S(1)}, f32[16,135]{1,0:T(8,128)S(1)}, u32[]{:S(2)}, u32[]{:S(2)}) collective-permute-start(f32[16,135]{1,0:T(8,128)S(1)} %shard_map.134), channel_id=1, source_target_pairs={{2,0},{3,1},{0,2},{1,3},{6,4},{7,5},{4,6},{5,7},{10,8},{11,9},{8,1... | collective-permute-start | bytes 25928 | tf_op jit(solution)/shard_map/ppermute | solution.py:511
  79.4 1.9 collective-permute-done.77
  83.9 8.6 %shard_map.135 = (f32[7,135,16,128]{3,2,1,0:T(8,128)S(1)}, f32[135,16,128]{2,1,0:T(8,128)S(1)}, f32[1,128]{1,0:T(1,128)}) custom-call(f32[7,135,16,135]{3,2,1,0:T(8,128)} %bitcast.47, f32[16,135]{1,0:T(8,128)S(1)} %get-tuple-element.191.refs_1_.refs_5_.refs_2_), custom_call_target="tpu_custom_call" | custom-call | tf_op jit(solution)/shard_map/pallas_call | solution.py:47
  94.4 2.7 collective-permute-start.85
  102.9 1.9 collective-permute-done.87.refs_0_
  107.8 2.9 collective-permute-start.90
  111.4 1.8 collective-permute-done.90
  116.5 1.9 collective-permute-start.92
  120.0 3.1 collective-permute-done.93.refs_1_
  126.5 2.7 collective-permute-start.97
  135.0 1.9 collective-permute-done.99.refs_0_
  139.6 2.7 collective-permute-start.102
  146.1 2.1 collective-permute-start.107
  150.7 3.8 %collective-permute-done.105.refs_1_ = f32[64,135]{1,0:T(8,128)S(1)} collective-permute-done((f32[64,135]{1,0:T(8,128)S(1)}, f32[64,135]{1,0:T(8,128)S(1)}, u32[]{:S(2)}, u32[]{:S(2)}) %collective-permute-start.105) | collective-permute-done | bytes 34592 | tf_op jit(solution)/shard_map/ppermute | solution.py:511
  157.9 2.7 collective-permute-start.109
  166.3 1.9 collective-permute-done.111.refs_0_
  170.9 2.7 collective-permute-start.114
  177.4 2.1 collective-permute-start.119
  180.0 1.8 collective-permute-done.119.refs_4_
  182.0 3.4 collective-permute-done.117.refs_1_
  188.8 2.9 collective-permute-start.121
  197.4 1.9 collective-permute-done.123.refs_0_
  202.0 2.7 collective-permute-start.126
  208.5 2.1 collective-permute-start.131
  211.1 1.8 collective-permute-done.131.refs_4_
  213.1 3.4 collective-permute-done.129.refs_1_
  220.0 2.7 collective-permute-start.133
  228.4 2.1 collective-permute-done.135.refs_0_
  233.2 2.7 collective-permute-start.138
  239.7 2.5 collective-permute-start.143
  244.7 3.7 collective-permute-done.141.refs_1_
  252.4 2.7 collective-permute-start.145
  260.8 2.0 collective-permute-done.147.refs_0_
  265.2 2.7 collective-permute-start.150
  272.0 3.9 %collective-permute-start.155 = (f32[64,135]{1,0:T(8,128)S(1)}, f32[64,135]{1,0:T(8,128)S(1)}, u32[]{:S(2)}, u32[]{:S(2)}) collective-permute-start(f32[64,135]{1,0:T(8,128)S(1)} %pad_maximum_fusion.14.refs_2_), channel_id=1, source_target_pairs={{8,0},{9,1},{10,2},{11,3},{12,4},{13,5},{14,6},{15,7},{16,8},{17,9... | collective-permute-start | bytes 103688 | tf_op jit(solution)/shard_map/ppermute | solution.py:511
  278.4 3.7 collective-permute-done.153.refs_1_
  286.1 2.7 collective-permute-start.157
  294.6 2.0 collective-permute-done.159.refs_0_
  299.0 2.3 collective-permute-start.162
  305.1 3.9 %collective-permute-start.167 = (f32[64,135]{1,0:T(8,128)S(1)}, f32[64,135]{1,0:T(8,128)S(1)}, u32[]{:S(2)}, u32[]{:S(2)}) collective-permute-start(f32[64,135]{1,0:T(8,128)S(1)} %pad_maximum_fusion.16.refs_2_), channel_id=1, source_target_pairs={{8,0},{9,1},{10,2},{11,3},{12,4},{13,5},{14,6},{15,7},{16,8},{17,9... | collective-permute-start | bytes 103688 | tf_op jit(solution)/shard_map/ppermute | solution.py:511
  311.5 3.8 %collective-permute-done.165.refs_1_ = f32[64,135]{1,0:T(8,128)S(1)} collective-permute-done((f32[64,135]{1,0:T(8,128)S(1)}, f32[64,135]{1,0:T(8,128)S(1)}, u32[]{:S(2)}, u32[]{:S(2)}) %collective-permute-start.165) | collective-permute-done | bytes 34592 | tf_op jit(solution)/shard_map/ppermute | solution.py:511
  316.7 1.8 shard_map.150
  318.5 2.4 collective-permute-start.170
  323.5 2.6 collective-permute-done.169
  330.0 7.3 %collective-permute-start.176 = (f32[16,128]{1,0:T(8,128)S(1)}, f32[16,128]{1,0:T(8,128)S(1)}, u32[]{:S(2)}, u32[]{:S(2)}) collective-permute-start(f32[16,128]{1,0:T(8,128)S(1)} %add_add_fusion.14), channel_id=1, source_target_pairs={{48,0},{49,1},{50,2},{51,3},{52,4},{53,5},{54,6},{55,7},{56,8},{57... | collective-permute-start | bytes 24584 | tf_op jit(solution)/shard_map/ppermute | solution.py:528
  337.3 8.4 %collective-permute-start.175 = (f32[16,128]{1,0:T(8,128)S(1)}, f32[16,128]{1,0:T(8,128)S(1)}, u32[]{:S(2)}, u32[]{:S(2)}) collective-permute-start(f32[16,128]{1,0:T(8,128)S(1)} %add_add_fusion.14), channel_id=1, source_target_pairs={{32,0},{33,1},{34,2},{35,3},{36,4},{37,5},{38,6},{39,7},{40,8},{41... | collective-permute-start | bytes 24584 | tf_op jit(solution)/shard_map/ppermute | solution.py:528
  345.7 2.9 collective-permute-start.174
  348.6 2.3 collective-permute-done.174
  350.9 7.1 %collective-permute-start.179 = (f32[16,128]{1,0:T(8,128)S(1)}, f32[16,128]{1,0:T(8,128)S(1)}, u32[]{:S(2)}, u32[]{:S(2)}) collective-permute-start(f32[16,128]{1,0:T(8,128)S(1)} %add_add_fusion.13), channel_id=1, source_target_pairs={{192,0},{193,1},{194,2},{195,3},{196,4},{197,5},{198,6},{199,7},{2... | collective-permute-start | bytes 24584 | tf_op jit(solution)/shard_map/ppermute | solution.py:528
  358.0 2.2 collective-permute-start.178
  360.5 5.1 %collective-permute-done.178 = f32[16,128]{1,0:T(8,128)S(1)} collective-permute-done((f32[16,128]{1,0:T(8,128)S(1)}, f32[16,128]{1,0:T(8,128)S(1)}, u32[]{:S(2)}, u32[]{:S(2)}) %collective-permute-start.178) | collective-permute-done | bytes 8224 | tf_op jit(solution)/shard_map/ppermute | solution.py:528
  365.6 4.3 %shard_map.151 = (f32[9,16,135]{2,1,0:T(8,128)}, f32[8,128]{1,0:T(8,128)}, f32[1,128]{1,0:T(1,128)S(1)}, f32[1,128]{1,0:T(1,128)S(1)}) custom-call(f32[16,128]{1,0:T(8,128)S(1)} %add_add_fusion.12.refs_0_, f32[1,128]{1,0:T(1,128)S(1)} %add_add_fusion.17.parts_ref.refs_6_.refs_14_.refs_1_, f32[16,135]{1,0:T(8,128)S(1)} %get-tuple-element.191.refs_1_.refs_5_.refs_2_, ...), custom_call_target="tpu_custom_call" | custom-call | tf_op jit(solution)/shard_map/pallas_call | solution.py:47
  (285 shorter events, 158.1 us)
Async XLA Ops:
  2.0 12.4 %collective-permute-start.62 = (f32[1,128]{1,0:T(1,128)S(1)}, f32[1,128]{1,0:T(1,128)S(1)}, u32[]{:S(2)}, u32[]{:S(2)}) collective-permute-start(f32[1,128]{1,0:T(1,128)S(1)} %shard_map.129), channel_id=1, source_target_pairs={{3,0},{2,1},{1,2},{0,3},{7,4},{6,5},{5,6},{4,7},{11,8},{10,9},{9,1... | collective-permute-start | bytes 1544 | tf_op jit(solution)/shard_map/ppermute | solution.py:528
  5.1 9.3 %collective-permute-start.61 = (f32[1,128]{1,0:T(1,128)S(1)}, f32[1,128]{1,0:T(1,128)S(1)}, u32[]{:S(2)}, u32[]{:S(2)}) collective-permute-start(f32[1,128]{1,0:T(1,128)S(1)} %shard_map.129), channel_id=1, source_target_pairs={{2,0},{3,1},{0,2},{1,3},{6,4},{7,5},{4,6},{5,7},{10,8},{11,9},{8,1... | collective-permute-start | bytes 1544 | tf_op jit(solution)/shard_map/ppermute | solution.py:528
  5.7 8.7 %collective-permute-start.60 = (f32[1,128]{1,0:T(1,128)S(1)}, f32[1,128]{1,0:T(1,128)S(1)}, u32[]{:S(2)}, u32[]{:S(2)}) collective-permute-start(f32[1,128]{1,0:T(1,128)S(1)} %shard_map.129), channel_id=1, source_target_pairs={{1,0},{0,1},{3,2},{2,3},{5,4},{4,5},{7,6},{6,7},{9,8},{8,9},{11,10... | collective-permute-start | bytes 1544 | tf_op jit(solution)/shard_map/ppermute | solution.py:528
  18.2 19.3 %collective-permute-start.68 = (f32[1,128]{1,0:T(1,128)S(1)}, f32[1,128]{1,0:T(1,128)S(1)}, u32[]{:S(2)}, u32[]{:S(2)}) collective-permute-start(f32[1,128]{1,0:T(1,128)S(1)} %add_add_fusion.19.refs_3_), channel_id=1, source_target_pairs={{48,0},{49,1},{50,2},{51,3},{52,4},{53,5},{54,6},{55,7},{56,8},{57... | collective-permute-start | bytes 1544 | tf_op jit(solution)/shard_map/ppermute | solution.py:528
  20.3 17.2 %collective-permute-start.67 = (f32[1,128]{1,0:T(1,128)S(1)}, f32[1,128]{1,0:T(1,128)S(1)}, u32[]{:S(2)}, u32[]{:S(2)}) collective-permute-start(f32[1,128]{1,0:T(1,128)S(1)} %add_add_fusion.19.refs_3_), channel_id=1, source_target_pairs={{32,0},{33,1},{34,2},{35,3},{36,4},{37,5},{38,6},{39,7},{40,8},{41... | collective-permute-start | bytes 1544 | tf_op jit(solution)/shard_map/ppermute | solution.py:528
  20.4 17.1 %collective-permute-start.66 = (f32[1,128]{1,0:T(1,128)S(1)}, f32[1,128]{1,0:T(1,128)S(1)}, u32[]{:S(2)}, u32[]{:S(2)}) collective-permute-start(f32[1,128]{1,0:T(1,128)S(1)} %add_add_fusion.19.refs_3_), channel_id=1, source_target_pairs={{16,0},{17,1},{18,2},{19,3},{20,4},{21,5},{22,6},{23,7},{24,8},{25... | collective-permute-start | bytes 1544 | tf_op jit(solution)/shard_map/ppermute | solution.py:528
  37.5 20.6 %collective-permute-start.71 = (f32[1,128]{1,0:T(1,128)S(1)}, f32[1,128]{1,0:T(1,128)S(1)}, u32[]{:S(2)}, u32[]{:S(2)}) collective-permute-start(f32[1,128]{1,0:T(1,128)S(1)} %add_add_fusion.18.refs_3_), channel_id=1, source_target_pairs={{192,0},{193,1},{194,2},{195,3},{196,4},{197,5},{198,6},{199,7},{2... | collective-permute-start | bytes 1544 | tf_op jit(solution)/shard_map/ppermute | solution.py:528
  42.0 16.1 %collective-permute-start.70 = (f32[1,128]{1,0:T(1,128)S(1)}, f32[1,128]{1,0:T(1,128)S(1)}, u32[]{:S(2)}, u32[]{:S(2)}) collective-permute-start(f32[1,128]{1,0:T(1,128)S(1)} %add_add_fusion.18.refs_3_), channel_id=1, source_target_pairs={{128,0},{129,1},{130,2},{131,3},{132,4},{133,5},{134,6},{135,7},{1... | collective-permute-start | bytes 1544 | tf_op jit(solution)/shard_map/ppermute | solution.py:528
  43.0 15.1 %collective-permute-start.69 = (f32[1,128]{1,0:T(1,128)S(1)}, f32[1,128]{1,0:T(1,128)S(1)}, u32[]{:S(2)}, u32[]{:S(2)}) collective-permute-start(f32[1,128]{1,0:T(1,128)S(1)} %add_add_fusion.18.refs_3_), channel_id=1, source_target_pairs={{64,0},{65,1},{66,2},{67,3},{68,4},{69,5},{70,6},{71,7},{72,8},{73... | collective-permute-start | bytes 1544 | tf_op jit(solution)/shard_map/ppermute | solution.py:528
  59.0 8.2 %collective-permute-start.74 = (f32[16,135]{1,0:T(8,128)S(1)}, f32[16,135]{1,0:T(8,128)S(1)}, u32[]{:S(2)}, u32[]{:S(2)}) collective-permute-start(f32[16,135]{1,0:T(8,128)S(1)} %get-tuple-element.191.refs_1_.refs_5_.refs_2_), channel_id=1, source_target_pairs={{3,0},{0,1},{1,2},{2,3},{7,4},{4,5},{5,6},{6,7},{11,8},{8,9},{9,10... | collective-permute-start | bytes 25928 | tf_op jit(solution)/shard_map/ppermute | solution.py:511
  60.6 6.6 %collective-permute-start.73 = (f32[16,135]{1,0:T(8,128)S(1)}, f32[16,135]{1,0:T(8,128)S(1)}, u32[]{:S(2)}, u32[]{:S(2)}) collective-permute-start(f32[16,135]{1,0:T(8,128)S(1)} %get-tuple-element.191.refs_1_.refs_5_.refs_2_), channel_id=1, source_target_pairs={{2,0},{3,1},{0,2},{1,3},{6,4},{7,5},{4,6},{5,7},{10,8},{11,9},{8,1... | collective-permute-start | bytes 25928 | tf_op jit(solution)/shard_map/ppermute | solution.py:511
  73.4 5.0 %collective-permute-start.79 = (f32[16,135]{1,0:T(8,128)S(1)}, f32[16,135]{1,0:T(8,128)S(1)}, u32[]{:S(2)}, u32[]{:S(2)}) collective-permute-start(f32[16,135]{1,0:T(8,128)S(1)} %shard_map.134), channel_id=1, source_target_pairs={{3,0},{0,1},{1,2},{2,3},{7,4},{4,5},{5,6},{6,7},{11,8},{8,9},{9,10... | collective-permute-start | bytes 25928 | tf_op jit(solution)/shard_map/ppermute | solution.py:511
  73.6 5.8 %collective-permute-start.78 = (f32[16,135]{1,0:T(8,128)S(1)}, f32[16,135]{1,0:T(8,128)S(1)}, u32[]{:S(2)}, u32[]{:S(2)}) collective-permute-start(f32[16,135]{1,0:T(8,128)S(1)} %shard_map.134), channel_id=1, source_target_pairs={{2,0},{3,1},{0,2},{1,3},{6,4},{7,5},{4,6},{5,7},{10,8},{11,9},{8,1... | collective-permute-start | bytes 25928 | tf_op jit(solution)/shard_map/ppermute | solution.py:511
  81.2 11.3 %collective-permute-start.83 = (f32[64,135]{1,0:T(8,128)S(1)}, f32[64,135]{1,0:T(8,128)S(1)}, u32[]{:S(2)}, u32[]{:S(2)}) collective-permute-start(f32[64,135]{1,0:T(8,128)S(1)} %pad_maximum_fusion.2.refs_2_), channel_id=1, source_target_pairs={{8,0},{9,1},{10,2},{11,3},{12,4},{13,5},{14,6},{15,7},{16,8},{17,9... | collective-permute-start | bytes 103688 | tf_op jit(solution)/shard_map/ppermute | solution.py:511
  81.8 10.7 %collective-permute-start.82 = (f32[64,135]{1,0:T(8,128)S(1)}, f32[64,135]{1,0:T(8,128)S(1)}, u32[]{:S(2)}, u32[]{:S(2)}) collective-permute-start(f32[64,135]{1,0:T(8,128)S(1)} %pad_maximum_fusion.2.refs_2_), channel_id=1, source_target_pairs={{4,0},{5,1},{6,2},{7,3},{8,4},{9,5},{10,6},{11,7},{12,8},{13,9},{1... | collective-permute-start | bytes 103688 | tf_op jit(solution)/shard_map/ppermute | solution.py:511
  81.8 10.7 %collective-permute-start.81 = (f32[64,135]{1,0:T(8,128)S(1)}, f32[64,135]{1,0:T(8,128)S(1)}, u32[]{:S(2)}, u32[]{:S(2)}) collective-permute-start(f32[64,135]{1,0:T(8,128)S(1)} %pad_maximum_fusion.2.refs_2_), channel_id=1, source_target_pairs={{252,0},{253,1},{254,2},{255,3},{0,4},{1,5},{2,6},{3,7},{4,8},{5,9... | collective-permute-start | bytes 103688 | tf_op jit(solution)/shard_map/ppermute | solution.py:511
  82.3 10.2 %collective-permute-start.80 = (f32[64,135]{1,0:T(8,128)S(1)}, f32[64,135]{1,0:T(8,128)S(1)}, u32[]{:S(2)}, u32[]{:S(2)}) collective-permute-start(f32[64,135]{1,0:T(8,128)S(1)} %pad_maximum_fusion.2.refs_2_), channel_id=1, source_target_pairs={{248,0},{249,1},{250,2},{251,3},{252,4},{253,5},{254,6},{255,7},{0... | collective-permute-start | bytes 103688 | tf_op jit(solution)/shard_map/ppermute | solution.py:511
  94.3 5.0 %collective-permute-start.86 = (f32[16,135]{1,0:T(8,128)S(1)}, f32[16,135]{1,0:T(8,128)S(1)}, u32[]{:S(2)}, u32[]{:S(2)}) collective-permute-start(f32[16,135]{1,0:T(8,128)S(1)} %shard_map.136.refs_5_.refs_6_.refs_3_), channel_id=1, source_target_pairs={{3,0},{0,1},{1,2},{2,3},{7,4},{4,5},{5,6},{6,7},{11,8},{8,9},{9,10... | collective-permute-start | bytes 25928 | tf_op jit(solution)/shard_map/ppermute | solution.py:511
  94.4 5.3 %collective-permute-start.85 = (f32[16,135]{1,0:T(8,128)S(1)}, f32[16,135]{1,0:T(8,128)S(1)}, u32[]{:S(2)}, u32[]{:S(2)}) collective-permute-start(f32[16,135]{1,0:T(8,128)S(1)} %shard_map.136.refs_5_.refs_6_.refs_3_), channel_id=1, source_target_pairs={{2,0},{3,1},{0,2},{1,3},{6,4},{7,5},{4,6},{5,7},{10,8},{11,9},{8,1... | collective-permute-start | bytes 25928 | tf_op jit(solution)/shard_map/ppermute | solution.py:511
  107.8 5.4 %collective-permute-start.90 = (f32[16,135]{1,0:T(8,128)S(1)}, f32[16,135]{1,0:T(8,128)S(1)}, u32[]{:S(2)}, u32[]{:S(2)}) collective-permute-start(f32[16,135]{1,0:T(8,128)S(1)} %shard_map.137), channel_id=1, source_target_pairs={{2,0},{3,1},{0,2},{1,3},{6,4},{7,5},{4,6},{5,7},{10,8},{11,9},{8,1... | collective-permute-start | bytes 25928 | tf_op jit(solution)/shard_map/ppermute | solution.py:511
  114.5 5.5 %collective-permute-start.95 = (f32[64,135]{1,0:T(8,128)S(1)}, f32[64,135]{1,0:T(8,128)S(1)}, u32[]{:S(2)}, u32[]{:S(2)}) collective-permute-start(f32[64,135]{1,0:T(8,128)S(1)} %pad_maximum_fusion.4.refs_2_), channel_id=1, source_target_pairs={{8,0},{9,1},{10,2},{11,3},{12,4},{13,5},{14,6},{15,7},{16,8},{17,9... | collective-permute-start | bytes 103688 | tf_op jit(solution)/shard_map/ppermute | solution.py:511
  115.9 7.2 %collective-permute-start.93 = (f32[64,135]{1,0:T(8,128)S(1)}, f32[64,135]{1,0:T(8,128)S(1)}, u32[]{:S(2)}, u32[]{:S(2)}) collective-permute-start(f32[64,135]{1,0:T(8,128)S(1)} %pad_maximum_fusion.4.refs_2_), channel_id=1, source_target_pairs={{252,0},{253,1},{254,2},{255,3},{0,4},{1,5},{2,6},{3,7},{4,8},{5,9... | collective-permute-start | bytes 103688 | tf_op jit(solution)/shard_map/ppermute | solution.py:511
  116.5 8.0 %collective-permute-start.92 = (f32[64,135]{1,0:T(8,128)S(1)}, f32[64,135]{1,0:T(8,128)S(1)}, u32[]{:S(2)}, u32[]{:S(2)}) collective-permute-start(f32[64,135]{1,0:T(8,128)S(1)} %pad_maximum_fusion.4.refs_2_), channel_id=1, source_target_pairs={{248,0},{249,1},{250,2},{251,3},{252,4},{253,5},{254,6},{255,7},{0... | collective-permute-start | bytes 103688 | tf_op jit(solution)/shard_map/ppermute | solution.py:511
  126.1 5.0 %collective-permute-start.98 = (f32[16,135]{1,0:T(8,128)S(1)}, f32[16,135]{1,0:T(8,128)S(1)}, u32[]{:S(2)}, u32[]{:S(2)}) collective-permute-start(f32[16,135]{1,0:T(8,128)S(1)} %shard_map.138.refs_5_.refs_7_.refs_4_), channel_id=1, source_target_pairs={{3,0},{0,1},{1,2},{2,3},{7,4},{4,5},{5,6},{6,7},{11,8},{8,9},{9,10... | collective-permute-start | bytes 25928 | tf_op jit(solution)/shard_map/ppermute | solution.py:511
  126.5 5.2 %collective-permute-start.97 = (f32[16,135]{1,0:T(8,128)S(1)}, f32[16,135]{1,0:T(8,128)S(1)}, u32[]{:S(2)}, u32[]{:S(2)}) collective-permute-start(f32[16,135]{1,0:T(8,128)S(1)} %shard_map.138.refs_5_.refs_7_.refs_4_), channel_id=1, source_target_pairs={{2,0},{3,1},{0,2},{1,3},{6,4},{7,5},{4,6},{5,7},{10,8},{11,9},{8,1... | collective-permute-start | bytes 25928 | tf_op jit(solution)/shard_map/ppermute | solution.py:511
  138.5 5.0 %collective-permute-start.103 = (f32[16,135]{1,0:T(8,128)S(1)}, f32[16,135]{1,0:T(8,128)S(1)}, u32[]{:S(2)}, u32[]{:S(2)}) collective-permute-start(f32[16,135]{1,0:T(8,128)S(1)} %shard_map.139), channel_id=1, source_target_pairs={{3,0},{0,1},{1,2},{2,3},{7,4},{4,5},{5,6},{6,7},{11,8},{8,9},{9,10... | collective-permute-start | bytes 25928 | tf_op jit(solution)/shard_map/ppermute | solution.py:511
  139.6 5.2 %collective-permute-start.102 = (f32[16,135]{1,0:T(8,128)S(1)}, f32[16,135]{1,0:T(8,128)S(1)}, u32[]{:S(2)}, u32[]{:S(2)}) collective-permute-start(f32[16,135]{1,0:T(8,128)S(1)} %shard_map.139), channel_id=1, source_target_pairs={{2,0},{3,1},{0,2},{1,3},{6,4},{7,5},{4,6},{5,7},{10,8},{11,9},{8,1... | collective-permute-start | bytes 25928 | tf_op jit(solution)/shard_map/ppermute | solution.py:511
  148.2 6.3 %collective-permute-start.105 = (f32[64,135]{1,0:T(8,128)S(1)}, f32[64,135]{1,0:T(8,128)S(1)}, u32[]{:S(2)}, u32[]{:S(2)}) collective-permute-start(f32[64,135]{1,0:T(8,128)S(1)} %pad_maximum_fusion.6.refs_2_), channel_id=1, source_target_pairs={{252,0},{253,1},{254,2},{255,3},{0,4},{1,5},{2,6},{3,7},{4,8},{5,9... | collective-permute-start | bytes 103688 | tf_op jit(solution)/shard_map/ppermute | solution.py:511
  149.1 6.7 %collective-permute-start.104 = (f32[64,135]{1,0:T(8,128)S(1)}, f32[64,135]{1,0:T(8,128)S(1)}, u32[]{:S(2)}, u32[]{:S(2)}) collective-permute-start(f32[64,135]{1,0:T(8,128)S(1)} %pad_maximum_fusion.6.refs_2_), channel_id=1, source_target_pairs={{248,0},{249,1},{250,2},{251,3},{252,4},{253,5},{254,6},{255,7},{0... | collective-permute-start | bytes 103688 | tf_op jit(solution)/shard_map/ppermute | solution.py:511
  157.5 5.0 %collective-permute-start.110 = (f32[16,135]{1,0:T(8,128)S(1)}, f32[16,135]{1,0:T(8,128)S(1)}, u32[]{:S(2)}, u32[]{:S(2)}) collective-permute-start(f32[16,135]{1,0:T(8,128)S(1)} %shard_map.140.refs_5_.refs_8_), channel_id=1, source_target_pairs={{3,0},{0,1},{1,2},{2,3},{7,4},{4,5},{5,6},{6,7},{11,8},{8,9},{9,10... | collective-permute-start | bytes 25928 | tf_op jit(solution)/shard_map/ppermute | solution.py:511
  157.9 5.2 %collective-permute-start.109 = (f32[16,135]{1,0:T(8,128)S(1)}, f32[16,135]{1,0:T(8,128)S(1)}, u32[]{:S(2)}, u32[]{:S(2)}) collective-permute-start(f32[16,135]{1,0:T(8,128)S(1)} %shard_map.140.refs_5_.refs_8_), channel_id=1, source_target_pairs={{2,0},{3,1},{0,2},{1,3},{6,4},{7,5},{4,6},{5,7},{10,8},{11,9},{8,1... | collective-permute-start | bytes 25928 | tf_op jit(solution)/shard_map/ppermute | solution.py:511
  170.9 5.2 %collective-permute-start.114 = (f32[16,135]{1,0:T(8,128)S(1)}, f32[16,135]{1,0:T(8,128)S(1)}, u32[]{:S(2)}, u32[]{:S(2)}) collective-permute-start(f32[16,135]{1,0:T(8,128)S(1)} %shard_map.141), channel_id=1, source_target_pairs={{2,0},{3,1},{0,2},{1,3},{6,4},{7,5},{4,6},{5,7},{10,8},{11,9},{8,1... | collective-permute-start | bytes 25928 | tf_op jit(solution)/shard_map/ppermute | solution.py:511
  179.5 5.9 %collective-permute-start.117 = (f32[64,135]{1,0:T(8,128)S(1)}, f32[64,135]{1,0:T(8,128)S(1)}, u32[]{:S(2)}, u32[]{:S(2)}) collective-permute-start(f32[64,135]{1,0:T(8,128)S(1)} %pad_maximum_fusion.8.refs_2_), channel_id=1, source_target_pairs={{252,0},{253,1},{254,2},{255,3},{0,4},{1,5},{2,6},{3,7},{4,8},{5,9... | collective-permute-start | bytes 103688 | tf_op jit(solution)/shard_map/ppermute | solution.py:511
  180.0 6.7 %collective-permute-start.116 = (f32[64,135]{1,0:T(8,128)S(1)}, f32[64,135]{1,0:T(8,128)S(1)}, u32[]{:S(2)}, u32[]{:S(2)}) collective-permute-start(f32[64,135]{1,0:T(8,128)S(1)} %pad_maximum_fusion.8.refs_2_), channel_id=1, source_target_pairs={{248,0},{249,1},{250,2},{251,3},{252,4},{253,5},{254,6},{255,7},{0... | collective-permute-start | bytes 103688 | tf_op jit(solution)/shard_map/ppermute | solution.py:511
  188.4 5.0 %collective-permute-start.122 = (f32[16,135]{1,0:T(8,128)S(1)}, f32[16,135]{1,0:T(8,128)S(1)}, u32[]{:S(2)}, u32[]{:S(2)}) collective-permute-start(f32[16,135]{1,0:T(8,128)S(1)} %shard_map.142.refs_5_.refs_9_.refs_6_), channel_id=1, source_target_pairs={{3,0},{0,1},{1,2},{2,3},{7,4},{4,5},{5,6},{6,7},{11,8},{8,9},{9,10... | collective-permute-start | bytes 25928 | tf_op jit(solution)/shard_map/ppermute | solution.py:511
  188.8 5.4 %collective-permute-start.121 = (f32[16,135]{1,0:T(8,128)S(1)}, f32[16,135]{1,0:T(8,128)S(1)}, u32[]{:S(2)}, u32[]{:S(2)}) collective-permute-start(f32[16,135]{1,0:T(8,128)S(1)} %shard_map.142.refs_5_.refs_9_.refs_6_), channel_id=1, source_target_pairs={{2,0},{3,1},{0,2},{1,3},{6,4},{7,5},{4,6},{5,7},{10,8},{11,9},{8,1... | collective-permute-start | bytes 25928 | tf_op jit(solution)/shard_map/ppermute | solution.py:511
  201.0 5.0 %collective-permute-start.127 = (f32[16,135]{1,0:T(8,128)S(1)}, f32[16,135]{1,0:T(8,128)S(1)}, u32[]{:S(2)}, u32[]{:S(2)}) collective-permute-start(f32[16,135]{1,0:T(8,128)S(1)} %shard_map.143), channel_id=1, source_target_pairs={{3,0},{0,1},{1,2},{2,3},{7,4},{4,5},{5,6},{6,7},{11,8},{8,9},{9,10... | collective-permute-start | bytes 25928 | tf_op jit(solution)/shard_map/ppermute | solution.py:511
  202.0 5.2 %collective-permute-start.126 = (f32[16,135]{1,0:T(8,128)S(1)}, f32[16,135]{1,0:T(8,128)S(1)}, u32[]{:S(2)}, u32[]{:S(2)}) collective-permute-start(f32[16,135]{1,0:T(8,128)S(1)} %shard_map.143), channel_id=1, source_target_pairs={{2,0},{3,1},{0,2},{1,3},{6,4},{7,5},{4,6},{5,7},{10,8},{11,9},{8,1... | collective-permute-start | bytes 25928 | tf_op jit(solution)/shard_map/ppermute | solution.py:511
  210.6 5.9 %collective-permute-start.129 = (f32[64,135]{1,0:T(8,128)S(1)}, f32[64,135]{1,0:T(8,128)S(1)}, u32[]{:S(2)}, u32[]{:S(2)}) collective-permute-start(f32[64,135]{1,0:T(8,128)S(1)} %pad_maximum_fusion.10.refs_2_), channel_id=1, source_target_pairs={{252,0},{253,1},{254,2},{255,3},{0,4},{1,5},{2,6},{3,7},{4,8},{5,9... | collective-permute-start | bytes 103688 | tf_op jit(solution)/shard_map/ppermute | solution.py:511
  211.1 6.7 %collective-permute-start.128 = (f32[64,135]{1,0:T(8,128)S(1)}, f32[64,135]{1,0:T(8,128)S(1)}, u32[]{:S(2)}, u32[]{:S(2)}) collective-permute-start(f32[64,135]{1,0:T(8,128)S(1)} %pad_maximum_fusion.10.refs_2_), channel_id=1, source_target_pairs={{248,0},{249,1},{250,2},{251,3},{252,4},{253,5},{254,6},{255,7},{0... | collective-permute-start | bytes 103688 | tf_op jit(solution)/shard_map/ppermute | solution.py:511
  219.6 5.0 %collective-permute-start.134 = (f32[16,135]{1,0:T(8,128)S(1)}, f32[16,135]{1,0:T(8,128)S(1)}, u32[]{:S(2)}, u32[]{:S(2)}) collective-permute-start(f32[16,135]{1,0:T(8,128)S(1)} %shard_map.144.refs_5_.refs_10_.refs_7_), channel_id=1, source_target_pairs={{3,0},{0,1},{1,2},{2,3},{7,4},{4,5},{5,6},{6,7},{11,8},{8,9},{9,10... | collective-permute-start | bytes 25928 | tf_op jit(solution)/shard_map/ppermute | solution.py:511
  220.0 5.2 %collective-permute-start.133 = (f32[16,135]{1,0:T(8,128)S(1)}, f32[16,135]{1,0:T(8,128)S(1)}, u32[]{:S(2)}, u32[]{:S(2)}) collective-permute-start(f32[16,135]{1,0:T(8,128)S(1)} %shard_map.144.refs_5_.refs_10_.refs_7_), channel_id=1, source_target_pairs={{2,0},{3,1},{0,2},{1,3},{6,4},{7,5},{4,6},{5,7},{10,8},{11,9},{8,1... | collective-permute-start | bytes 25928 | tf_op jit(solution)/shard_map/ppermute | solution.py:511
  233.2 5.2 %collective-permute-start.138 = (f32[16,135]{1,0:T(8,128)S(1)}, f32[16,135]{1,0:T(8,128)S(1)}, u32[]{:S(2)}, u32[]{:S(2)}) collective-permute-start(f32[16,135]{1,0:T(8,128)S(1)} %shard_map.145), channel_id=1, source_target_pairs={{2,0},{3,1},{0,2},{1,3},{6,4},{7,5},{4,6},{5,7},{10,8},{11,9},{8,1... | collective-permute-start | bytes 25928 | tf_op jit(solution)/shard_map/ppermute | solution.py:511
  242.2 6.2 %collective-permute-start.141 = (f32[64,135]{1,0:T(8,128)S(1)}, f32[64,135]{1,0:T(8,128)S(1)}, u32[]{:S(2)}, u32[]{:S(2)}) collective-permute-start(f32[64,135]{1,0:T(8,128)S(1)} %pad_maximum_fusion.12.refs_2_), channel_id=1, source_target_pairs={{252,0},{253,1},{254,2},{255,3},{0,4},{1,5},{2,6},{3,7},{4,8},{5,9... | collective-permute-start | bytes 103688 | tf_op jit(solution)/shard_map/ppermute | solution.py:511
  242.7 7.0 %collective-permute-start.140 = (f32[64,135]{1,0:T(8,128)S(1)}, f32[64,135]{1,0:T(8,128)S(1)}, u32[]{:S(2)}, u32[]{:S(2)}) collective-permute-start(f32[64,135]{1,0:T(8,128)S(1)} %pad_maximum_fusion.12.refs_2_), channel_id=1, source_target_pairs={{248,0},{249,1},{250,2},{251,3},{252,4},{253,5},{254,6},{255,7},{0... | collective-permute-start | bytes 103688 | tf_op jit(solution)/shard_map/ppermute | solution.py:511
  251.4 5.0 %collective-permute-start.146 = (f32[16,135]{1,0:T(8,128)S(1)}, f32[16,135]{1,0:T(8,128)S(1)}, u32[]{:S(2)}, u32[]{:S(2)}) collective-permute-start(f32[16,135]{1,0:T(8,128)S(1)} %shard_map.146.refs_5_.refs_11_.refs_8_), channel_id=1, source_target_pairs={{3,0},{0,1},{1,2},{2,3},{7,4},{4,5},{5,6},{6,7},{11,8},{8,9},{9,10... | collective-permute-start | bytes 25928 | tf_op jit(solution)/shard_map/ppermute | solution.py:511
  252.4 5.2 %collective-permute-start.145 = (f32[16,135]{1,0:T(8,128)S(1)}, f32[16,135]{1,0:T(8,128)S(1)}, u32[]{:S(2)}, u32[]{:S(2)}) collective-permute-start(f32[16,135]{1,0:T(8,128)S(1)} %shard_map.146.refs_5_.refs_11_.refs_8_), channel_id=1, source_target_pairs={{2,0},{3,1},{0,2},{1,3},{6,4},{7,5},{4,6},{5,7},{10,8},{11,9},{8,1... | collective-permute-start | bytes 25928 | tf_op jit(solution)/shard_map/ppermute | solution.py:511
  265.2 5.2 %collective-permute-start.150 = (f32[16,135]{1,0:T(8,128)S(1)}, f32[16,135]{1,0:T(8,128)S(1)}, u32[]{:S(2)}, u32[]{:S(2)}) collective-permute-start(f32[16,135]{1,0:T(8,128)S(1)} %shard_map.147), channel_id=1, source_target_pairs={{2,0},{3,1},{0,2},{1,3},{6,4},{7,5},{4,6},{5,7},{10,8},{11,9},{8,1... | collective-permute-start | bytes 25928 | tf_op jit(solution)/shard_map/ppermute | solution.py:511
  272.0 5.8 %collective-permute-start.155 = (f32[64,135]{1,0:T(8,128)S(1)}, f32[64,135]{1,0:T(8,128)S(1)}, u32[]{:S(2)}, u32[]{:S(2)}) collective-permute-start(f32[64,135]{1,0:T(8,128)S(1)} %pad_maximum_fusion.14.refs_2_), channel_id=1, source_target_pairs={{8,0},{9,1},{10,2},{11,3},{12,4},{13,5},{14,6},{15,7},{16,8},{17,9... | collective-permute-start | bytes 103688 | tf_op jit(solution)/shard_map/ppermute | solution.py:511
  275.9 6.2 %collective-permute-start.153 = (f32[64,135]{1,0:T(8,128)S(1)}, f32[64,135]{1,0:T(8,128)S(1)}, u32[]{:S(2)}, u32[]{:S(2)}) collective-permute-start(f32[64,135]{1,0:T(8,128)S(1)} %pad_maximum_fusion.14.refs_2_), channel_id=1, source_target_pairs={{252,0},{253,1},{254,2},{255,3},{0,4},{1,5},{2,6},{3,7},{4,8},{5,9... | collective-permute-start | bytes 103688 | tf_op jit(solution)/shard_map/ppermute | solution.py:511
  276.4 7.0 %collective-permute-start.152 = (f32[64,135]{1,0:T(8,128)S(1)}, f32[64,135]{1,0:T(8,128)S(1)}, u32[]{:S(2)}, u32[]{:S(2)}) collective-permute-start(f32[64,135]{1,0:T(8,128)S(1)} %pad_maximum_fusion.14.refs_2_), channel_id=1, source_target_pairs={{248,0},{249,1},{250,2},{251,3},{252,4},{253,5},{254,6},{255,7},{0... | collective-permute-start | bytes 103688 | tf_op jit(solution)/shard_map/ppermute | solution.py:511
  285.1 5.0 %collective-permute-start.158 = (f32[16,135]{1,0:T(8,128)S(1)}, f32[16,135]{1,0:T(8,128)S(1)}, u32[]{:S(2)}, u32[]{:S(2)}) collective-permute-start(f32[16,135]{1,0:T(8,128)S(1)} %shard_map.148.refs_12_.refs_13_.refs_9_), channel_id=1, source_target_pairs={{3,0},{0,1},{1,2},{2,3},{7,4},{4,5},{5,6},{6,7},{11,8},{8,9},{9,10... | collective-permute-start | bytes 25928 | tf_op jit(solution)/shard_map/ppermute | solution.py:511
  286.1 5.2 %collective-permute-start.157 = (f32[16,135]{1,0:T(8,128)S(1)}, f32[16,135]{1,0:T(8,128)S(1)}, u32[]{:S(2)}, u32[]{:S(2)}) collective-permute-start(f32[16,135]{1,0:T(8,128)S(1)} %shard_map.148.refs_12_.refs_13_.refs_9_), channel_id=1, source_target_pairs={{2,0},{3,1},{0,2},{1,3},{6,4},{7,5},{4,6},{5,7},{10,8},{11,9},{8,1... | collective-permute-start | bytes 25928 | tf_op jit(solution)/shard_map/ppermute | solution.py:511
  299.0 5.2 %collective-permute-start.162 = (f32[16,135]{1,0:T(8,128)S(1)}, f32[16,135]{1,0:T(8,128)S(1)}, u32[]{:S(2)}, u32[]{:S(2)}) collective-permute-start(f32[16,135]{1,0:T(8,128)S(1)} %shard_map.149), channel_id=1, source_target_pairs={{2,0},{3,1},{0,2},{1,3},{6,4},{7,5},{4,6},{5,7},{10,8},{11,9},{8,1... | collective-permute-start | bytes 25928 | tf_op jit(solution)/shard_map/ppermute | solution.py:511
  305.1 5.8 %collective-permute-start.167 = (f32[64,135]{1,0:T(8,128)S(1)}, f32[64,135]{1,0:T(8,128)S(1)}, u32[]{:S(2)}, u32[]{:S(2)}) collective-permute-start(f32[64,135]{1,0:T(8,128)S(1)} %pad_maximum_fusion.16.refs_2_), channel_id=1, source_target_pairs={{8,0},{9,1},{10,2},{11,3},{12,4},{13,5},{14,6},{15,7},{16,8},{17,9... | collective-permute-start | bytes 103688 | tf_op jit(solution)/shard_map/ppermute | solution.py:511
  309.0 6.3 %collective-permute-start.165 = (f32[64,135]{1,0:T(8,128)S(1)}, f32[64,135]{1,0:T(8,128)S(1)}, u32[]{:S(2)}, u32[]{:S(2)}) collective-permute-start(f32[64,135]{1,0:T(8,128)S(1)} %pad_maximum_fusion.16.refs_2_), channel_id=1, source_target_pairs={{252,0},{253,1},{254,2},{255,3},{0,4},{1,5},{2,6},{3,7},{4,8},{5,9... | collective-permute-start | bytes 103688 | tf_op jit(solution)/shard_map/ppermute | solution.py:511
  309.5 7.2 %collective-permute-start.164 = (f32[64,135]{1,0:T(8,128)S(1)}, f32[64,135]{1,0:T(8,128)S(1)}, u32[]{:S(2)}, u32[]{:S(2)}) collective-permute-start(f32[64,135]{1,0:T(8,128)S(1)} %pad_maximum_fusion.16.refs_2_), channel_id=1, source_target_pairs={{248,0},{249,1},{250,2},{251,3},{252,4},{253,5},{254,6},{255,7},{0... | collective-permute-start | bytes 103688 | tf_op jit(solution)/shard_map/ppermute | solution.py:511
  321.0 5.2 %collective-permute-start.169 = (f32[16,128]{1,0:T(8,128)S(1)}, f32[16,128]{1,0:T(8,128)S(1)}, u32[]{:S(2)}, u32[]{:S(2)}) collective-permute-start(f32[16,128]{1,0:T(8,128)S(1)} %get-tuple-element.198), channel_id=1, source_target_pairs={{2,0},{3,1},{0,2},{1,3},{6,4},{7,5},{4,6},{5,7},{10,8},{11,9},{8,1... | collective-permute-start | bytes 24584 | tf_op jit(solution)/shard_map/ppermute | solution.py:528
  330.0 18.6 %collective-permute-start.176 = (f32[16,128]{1,0:T(8,128)S(1)}, f32[16,128]{1,0:T(8,128)S(1)}, u32[]{:S(2)}, u32[]{:S(2)}) collective-permute-start(f32[16,128]{1,0:T(8,128)S(1)} %add_add_fusion.14), channel_id=1, source_target_pairs={{48,0},{49,1},{50,2},{51,3},{52,4},{53,5},{54,6},{55,7},{56,8},{57... | collective-permute-start | bytes 24584 | tf_op jit(solution)/shard_map/ppermute | solution.py:528
  337.3 11.2 %collective-permute-start.175 = (f32[16,128]{1,0:T(8,128)S(1)}, f32[16,128]{1,0:T(8,128)S(1)}, u32[]{:S(2)}, u32[]{:S(2)}) collective-permute-start(f32[16,128]{1,0:T(8,128)S(1)} %add_add_fusion.14), channel_id=1, source_target_pairs={{32,0},{33,1},{34,2},{35,3},{36,4},{37,5},{38,6},{39,7},{40,8},{41... | collective-permute-start | bytes 24584 | tf_op jit(solution)/shard_map/ppermute | solution.py:528
  345.7 5.2 %collective-permute-start.174 = (f32[16,128]{1,0:T(8,128)S(1)}, f32[16,128]{1,0:T(8,128)S(1)}, u32[]{:S(2)}, u32[]{:S(2)}) collective-permute-start(f32[16,128]{1,0:T(8,128)S(1)} %add_add_fusion.14), channel_id=1, source_target_pairs={{16,0},{17,1},{18,2},{19,3},{20,4},{21,5},{22,6},{23,7},{24,8},{25... | collective-permute-start | bytes 24584 | tf_op jit(solution)/shard_map/ppermute | solution.py:528
  350.9 9.6 %collective-permute-start.179 = (f32[16,128]{1,0:T(8,128)S(1)}, f32[16,128]{1,0:T(8,128)S(1)}, u32[]{:S(2)}, u32[]{:S(2)}) collective-permute-start(f32[16,128]{1,0:T(8,128)S(1)} %add_add_fusion.13), channel_id=1, source_target_pairs={{192,0},{193,1},{194,2},{195,3},{196,4},{197,5},{198,6},{199,7},{2... | collective-permute-start | bytes 24584 | tf_op jit(solution)/shard_map/ppermute | solution.py:528
  358.0 7.6 %collective-permute-start.178 = (f32[16,128]{1,0:T(8,128)S(1)}, f32[16,128]{1,0:T(8,128)S(1)}, u32[]{:S(2)}, u32[]{:S(2)}) collective-permute-start(f32[16,128]{1,0:T(8,128)S(1)} %add_add_fusion.13), channel_id=1, source_target_pairs={{128,0},{129,1},{130,2},{131,3},{132,4},{133,5},{134,6},{135,7},{1... | collective-permute-start | bytes 24584 | tf_op jit(solution)/shard_map/ppermute | solution.py:528
  360.2 5.3 %collective-permute-start.177 = (f32[16,128]{1,0:T(8,128)S(1)}, f32[16,128]{1,0:T(8,128)S(1)}, u32[]{:S(2)}, u32[]{:S(2)}) collective-permute-start(f32[16,128]{1,0:T(8,128)S(1)} %add_add_fusion.13), channel_id=1, source_target_pairs={{64,0},{65,1},{66,2},{67,3},{68,4},{69,5},{70,6},{71,7},{72,8},{73... | collective-permute-start | bytes 24584 | tf_op jit(solution)/shard_map/ppermute | solution.py:528
  (74 other events, 443.6 us)
where the time goes:
time: 379 us; the launch traced here: 373 us
  starting transfers between devices  154 us (41%)
  waiting for transfers between devices  136 us (36%)
  Pallas kernels  65.9 us (17%)
  local copies, waits for them, and re-layouts  14.2 us (4%)
    ppermute x96, waiting for transfers between devices, shifted(): return lax.ppermute(array, ('dom', 'blk'), pairs)  121 us
    ppermute x96, starting transfers between devices, shifted(): return lax.ppermute(array, ('dom', 'blk'), pairs)  102 us
    pallas_call x23, Pallas kernels, call(): pl.pallas_call(body, out_shape=out_shape, in_specs=specs, out_specs=[spec...  65.9 us
    ppermute x24, starting transfers between devices, added(): lax.ppermute(part, ('dom', 'blk'), [(n ^ k * reach, n) for n in range(dev...  52.8 us
    ppermute x24, waiting for transfers between devices, added(): lax.ppermute(part, ('dom', 'blk'), [(n ^ k * reach, n) for n in range(dev...  14.4 us
  transfers between devices with their start and end apart: 120, of which 97 were waited for; matrix products, arithmetic and copies ran while one was open for 2% of the time, Pallas kernels for 9%

commit v1 on v0

--- a/solution.py
+++ b/solution.py
@@ -499,22 +499,31 @@
     norm_ref[...] = norms
 
 
-def shifted(array, d_dom, d_blk):
-    doms, blks = lax.axis_size("dom"), lax.axis_size("blk")
-    if d_dom == 0 and d_blk == 0:
+def shifted(array, step):
+    doms = lax.axis_size("dom")
+    if step == 0:
         return array
-    pairs = []
-    for d in range(doms):
-        for b in range(blks):
-            source = ((d + d_dom) % doms) * blks + (b + d_blk) % blks
-            pairs.append((source, d * blks + b))
-    return lax.ppermute(array, ("dom", "blk"), pairs)
+    return lax.ppermute(array, "dom", [((d + step) % doms, d) for d in range(doms)])
+
+
+def masks(blks):
+    return [2 * m - 1 for m in (1, 2, 4, 8) if m < blks]
+
+
+def row_order(blks):
+    order = [0]
+    for mask in masks(blks):
+        order = order + [o ^ mask for o in order]
+    return order
 
 
 def around(array, reach):
     blks = lax.axis_size("blk")
-    whole = jnp.concatenate([shifted(array, 0, b) for b in range(blks)], 0)
-    return [shifted(whole, d, 0) for d in range(-reach, reach + 1)]
+    whole = array
+    for mask in masks(blks):
+        other = lax.ppermute(whole, "blk", [(b ^ mask, b) for b in range(blks)])
+        whole = jnp.concatenate([whole, other], 0)
+    return [shifted(whole, d) for d in range(-reach, reach + 1)]
 
 
 def added(part, beside=()):
@@ -603,8 +612,8 @@
     rows = jax.ShapeDtypeStruct((elems, cols), f32)
 
     members = line_members.reshape(devices, elems)
-    near = jnp.array([(d, b) for d in range(-2, 3) for b in range(blks)], jnp.int32)
-    at = (dom + near[:, 0] + doms) % doms * blks + (blk + near[:, 1]) % blks
+    near = jnp.array([(d, o) for d in range(-2, 3) for o in row_order(blks)], jnp.int32)
+    at = (dom + near[:, 0] + doms) % doms * blks + (blk ^ near[:, 1])
     line_ids = members[at].reshape(-1)
     near_own = at[blks : 4 * blks]
     elem_ids = (near_own[:, None] * elems + jnp.arange(elems, dtype=jnp.int32)).reshape(-1)

time: 379 us -> 410 us (1.082)
  waiting for transfers between devices: 136 us -> 178 us
  starting transfers between devices: 154 us -> 137 us
  local copies, waits for them, and re-layouts: 14.2 us -> 20.8 us
    ppermute x96 -> x80, waiting for transfers between devices: 121 us -> 163 us  [the longest x32 90.9 us: around(): other = lax.ppermute(whole, 'blk', [(b ^ mask, b) for b in range(blks)])]
    ppermute x96 -> x80, starting transfers between devices: 102 us -> 83.2 us  [the longest x32 51.5 us: around(): other = lax.ppermute(whole, 'blk', [(b ^ mask, b) for b in range(blks)])]
    unnamed x41 -> x42, local copies, waits for them, and re-layouts: 5.8 us -> 12.4 us
  transfers between devices with their start and end apart: 120 -> 104, of which waited for: 97 -> 83; matrix products, arithmetic and copies ran while one was open for 2% -> 2% of each run, Pallas kernels for 9% -> 8%
where the time goes in v1:
time: 410 us; the launch traced here: 403 us
  waiting for transfers between devices  178 us (43%)
  starting transfers between devices  137 us (33%)
  Pallas kernels  64 us (16%)
  local copies, waits for them, and re-layouts  20.8 us (5%)
    ppermute x32, waiting for transfers between devices, around(): other = lax.ppermute(whole, 'blk', [(b ^ mask, b) for b in range(blks)])  90.9 us
    ppermute x48, waiting for transfers between devices, shifted(): lax.ppermute(array, 'dom', [((d + step) % doms, d) for d in range(doms)])  72.6 us
    pallas_call x23, Pallas kernels, call(): pl.pallas_call(body, out_shape=out_shape, in_specs=specs, out_specs=[spec...  64 us
    ppermute x24, starting transfers between devices, added(): lax.ppermute(part, ('dom', 'blk'), [(n ^ k * reach, n) for n in range(dev...  53.7 us
    ppermute x32, starting transfers between devices, around(): other = lax.ppermute(whole, 'blk', [(b ^ mask, b) for b in range(blks)])  51.5 us
    ppermute x48, starting transfers between devices, shifted(): lax.ppermute(array, 'dom', [((d + step) % doms, d) for d in range(doms)])  31.7 us
    ppermute x24, waiting for transfers between devices, added(): lax.ppermute(part, ('dom', 'blk'), [(n ^ k * reach, n) for n in range(dev...  15 us
    unnamed x42, local copies, waits for them, and re-layouts  12.4 us
  transfers between devices with their start and end apart: 104, of which 83 were waited for; matrix products, arithmetic and copies ran while one was open for 2% of the time, Pallas kernels for 8%

profile of v1, /device:TPU:68, one launch (start us, length us, event | category | flops | bytes accessed | tf_op | source)
XLA Modules:
  0.0 403.3 jit_solution(11308775472436030235)
XLA Ops:
  2.0 3.1 collective-permute-start.58
  6.6 2.6 reshape.103.refs_1_.refs_2_
  9.2 3.5 reshape.102.refs_0_.refs_1_
  20.3 3.0 collective-permute-start.62
  24.9 12.0 %shard_map.131 = (f32[8,1088,128]{2,1,0:T(8,128)S(1)}, f32[1088,128]{1,0:T(8,128)S(1)}, f32[1,128]{1,0:T(1,128)S(1)}) custom-call(f32[2,1080,135]{2,1,0:T(8,128)} %bitcast.42, f32[7,270,135]{2,1,0:T(8,128)S(1)} %copy-done.12, f32[7,270,135]{2,1,0:T(8,128)S(1)} %reshape.103.refs_1_.refs_2_, f32[1,128]{1,0:T(1,128)S(1)} %add_add_fusion.19.refs_3_), custom_call_target="tpu_custom_call" | custom-call | tf_op jit(solution)/shard_map/pallas_call | solution.py:47
  39.0 4.6 %collective-permute-start.67 = (f32[1,128]{1,0:T(1,128)S(1)}, f32[1,128]{1,0:T(1,128)S(1)}, u32[]{:S(2)}, u32[]{:S(2)}) collective-permute-start(f32[1,128]{1,0:T(1,128)S(1)} %add_add_fusion.18.refs_3_), channel_id=1, source_target_pairs={{192,0},{193,1},{194,2},{195,3},{196,4},{197,5},{198,6},{199,7},{2... | collective-permute-start | bytes 1544 | tf_op jit(solution)/shard_map/ppermute | solution.py:537
  46.1 10.2 %shard_map.132 = (f32[8,1088,128]{2,1,0:T(8,128)S(1)}, f32[1088,128]{1,0:T(8,128)S(1)}, f32[1,128]{1,0:T(1,128)S(1)}) custom-call(f32[2,1080,135]{2,1,0:T(8,128)S(1)} %bitcast.43, f32[7,270,135]{2,1,0:T(8,128)S(1)} %copy-done.12, f32[7,270,135]{2,1,0:T(8,128)S(1)} %reshape.103.refs_1_.refs_2_, f32[1,128]{1,0:T(1,128)S(1)} %add_add_fusion.18.refs_3_), custom_call_target="tpu_custom_call" | custom-call | tf_op jit(solution)/shard_map/pallas_call | solution.py:47
  62.9 3.0 collective-permute-start.69
  69.9 2.3 collective-permute-done.70.refs_0_
  72.2 2.3 copy-done.1
  74.4 2.3 copy-done.3
  78.8 3.4 collective-permute-done.72
  82.1 3.0 collective-permute-start.73
  90.0 8.6 %shard_map.135 = (f32[7,135,16,128]{3,2,1,0:T(8,128)S(1)}, f32[135,16,128]{2,1,0:T(8,128)S(1)}, f32[1,128]{1,0:T(1,128)}) custom-call(f32[7,135,16,135]{3,2,1,0:T(8,128)} %bitcast.39, f32[16,135]{1,0:T(8,128)S(1)} %get-tuple-element.191.refs_1_.refs_5_.refs_2_), custom_call_target="tpu_custom_call" | custom-call | tf_op jit(solution)/shard_map/pallas_call | solution.py:47
  100.4 3.7 collective-permute-done.78
  104.2 3.0 collective-permute-start.79
  114.9 3.7 collective-permute-done.82
  118.6 3.0 collective-permute-start.83
  129.5 2.5 collective-permute-done.85.refs_1_
  135.3 3.7 collective-permute-done.88
  139.0 2.9 collective-permute-start.89
  141.8 2.3 collective-permute-done.89
  149.7 3.7 collective-permute-done.92
  153.4 2.8 collective-permute-start.93
  156.3 2.3 collective-permute-done.93
  158.5 2.5 collective-permute-start.97
  163.6 3.4 collective-permute-done.95.refs_1_
  170.1 3.7 collective-permute-done.98
  173.8 3.1 collective-permute-start.99
  184.5 3.7 collective-permute-done.102
  188.3 3.4 collective-permute-start.103
  198.4 3.4 collective-permute-done.105.refs_1_
  204.9 3.7 collective-permute-done.108
  208.7 3.1 collective-permute-start.109
  219.3 3.7 collective-permute-done.112
  223.1 3.1 collective-permute-start.113
  232.8 3.4 collective-permute-done.115.refs_1_
  239.3 3.7 collective-permute-done.118
  243.1 3.2 collective-permute-start.119
  253.9 3.7 collective-permute-done.122
  257.7 3.1 collective-permute-start.123
  267.4 3.4 collective-permute-done.125.refs_1_
  273.9 3.7 collective-permute-done.128
  277.7 3.1 collective-permute-start.129
  288.4 3.7 collective-permute-done.132
  292.1 3.0 collective-permute-start.133
  297.3 3.8 collective-permute-start.137
  303.6 3.6 collective-permute-done.135.refs_1_
  310.3 3.7 collective-permute-done.138
  314.0 2.9 collective-permute-start.139
  321.1 2.5 collective-permute-done.140.refs_0_
  325.4 3.7 collective-permute-done.142
  329.1 3.0 collective-permute-start.143
  334.3 4.0 collective-permute-start.147
  340.7 3.4 collective-permute-done.145.refs_1_
  347.3 3.0 collective-permute-start.150
  352.2 3.2 collective-permute-done.149
  359.8 8.3 %collective-permute-start.156 = (f32[16,128]{1,0:T(8,128)S(1)}, f32[16,128]{1,0:T(8,128)S(1)}, u32[]{:S(2)}, u32[]{:S(2)}) collective-permute-start(f32[16,128]{1,0:T(8,128)S(1)} %add_add_fusion.14), channel_id=1, source_target_pairs={{48,0},{49,1},{50,2},{51,3},{52,4},{53,5},{54,6},{55,7},{56,8},{57... | collective-permute-start | bytes 24584 | tf_op jit(solution)/shard_map/ppermute | solution.py:537
  368.0 8.1 %collective-permute-start.155 = (f32[16,128]{1,0:T(8,128)S(1)}, f32[16,128]{1,0:T(8,128)S(1)}, u32[]{:S(2)}, u32[]{:S(2)}) collective-permute-start(f32[16,128]{1,0:T(8,128)S(1)} %add_add_fusion.14), channel_id=1, source_target_pairs={{32,0},{33,1},{34,2},{35,3},{36,4},{37,5},{38,6},{39,7},{40,8},{41... | collective-permute-start | bytes 24584 | tf_op jit(solution)/shard_map/ppermute | solution.py:537
  376.2 2.9 collective-permute-start.154
  379.0 2.3 collective-permute-done.154
  381.3 7.1 %collective-permute-start.159 = (f32[16,128]{1,0:T(8,128)S(1)}, f32[16,128]{1,0:T(8,128)S(1)}, u32[]{:S(2)}, u32[]{:S(2)}) collective-permute-start(f32[16,128]{1,0:T(8,128)S(1)} %add_add_fusion.13), channel_id=1, source_target_pairs={{192,0},{193,1},{194,2},{195,3},{196,4},{197,5},{198,6},{199,7},{2... | collective-permute-start | bytes 24584 | tf_op jit(solution)/shard_map/ppermute | solution.py:537
  390.9 5.1 %collective-permute-done.158 = f32[16,128]{1,0:T(8,128)S(1)} collective-permute-done((f32[16,128]{1,0:T(8,128)S(1)}, f32[16,128]{1,0:T(8,128)S(1)}, u32[]{:S(2)}, u32[]{:S(2)}) %collective-permute-start.158) | collective-permute-done | bytes 8224 | tf_op jit(solution)/shard_map/ppermute | solution.py:537
  396.0 4.3 %shard_map.151 = (f32[9,16,135]{2,1,0:T(8,128)}, f32[8,128]{1,0:T(8,128)}, f32[1,128]{1,0:T(1,128)S(1)}, f32[1,128]{1,0:T(1,128)S(1)}) custom-call(f32[16,128]{1,0:T(8,128)S(1)} %add_add_fusion.12.refs_0_, f32[1,128]{1,0:T(1,128)S(1)} %add_add_fusion.17.parts_ref.refs_6_.refs_14_.refs_1_, f32[16,135]{1,0:T(8,128)S(1)} %get-tuple-element.191.refs_1_.refs_5_.refs_2_, ...), custom_call_target="tpu_custom_call" | custom-call | tf_op jit(solution)/shard_map/pallas_call | solution.py:47
  (270 shorter events, 158.3 us)
Async XLA Ops:
  2.0 12.3 %collective-permute-start.58 = (f32[1,128]{1,0:T(1,128)S(1)}, f32[1,128]{1,0:T(1,128)S(1)}, u32[]{:S(2)}, u32[]{:S(2)}) collective-permute-start(f32[1,128]{1,0:T(1,128)S(1)} %shard_map.129), channel_id=1, source_target_pairs={{3,0},{2,1},{1,2},{0,3},{7,4},{6,5},{5,6},{4,7},{11,8},{10,9},{9,1... | collective-permute-start | bytes 1544 | tf_op jit(solution)/shard_map/ppermute | solution.py:537
  5.1 9.2 %collective-permute-start.57 = (f32[1,128]{1,0:T(1,128)S(1)}, f32[1,128]{1,0:T(1,128)S(1)}, u32[]{:S(2)}, u32[]{:S(2)}) collective-permute-start(f32[1,128]{1,0:T(1,128)S(1)} %shard_map.129), channel_id=1, source_target_pairs={{2,0},{3,1},{0,2},{1,3},{6,4},{7,5},{4,6},{5,7},{10,8},{11,9},{8,1... | collective-permute-start | bytes 1544 | tf_op jit(solution)/shard_map/ppermute | solution.py:537
  5.7 8.6 %collective-permute-start.56 = (f32[1,128]{1,0:T(1,128)S(1)}, f32[1,128]{1,0:T(1,128)S(1)}, u32[]{:S(2)}, u32[]{:S(2)}) collective-permute-start(f32[1,128]{1,0:T(1,128)S(1)} %shard_map.129), channel_id=1, source_target_pairs={{1,0},{0,1},{3,2},{2,3},{5,4},{4,5},{7,6},{6,7},{9,8},{8,9},{11,10... | collective-permute-start | bytes 1544 | tf_op jit(solution)/shard_map/ppermute | solution.py:537
  18.1 20.9 %collective-permute-start.64 = (f32[1,128]{1,0:T(1,128)S(1)}, f32[1,128]{1,0:T(1,128)S(1)}, u32[]{:S(2)}, u32[]{:S(2)}) collective-permute-start(f32[1,128]{1,0:T(1,128)S(1)} %add_add_fusion.19.refs_3_), channel_id=1, source_target_pairs={{48,0},{49,1},{50,2},{51,3},{52,4},{53,5},{54,6},{55,7},{56,8},{57... | collective-permute-start | bytes 1544 | tf_op jit(solution)/shard_map/ppermute | solution.py:537
  20.1 18.8 %collective-permute-start.63 = (f32[1,128]{1,0:T(1,128)S(1)}, f32[1,128]{1,0:T(1,128)S(1)}, u32[]{:S(2)}, u32[]{:S(2)}) collective-permute-start(f32[1,128]{1,0:T(1,128)S(1)} %add_add_fusion.19.refs_3_), channel_id=1, source_target_pairs={{32,0},{33,1},{34,2},{35,3},{36,4},{37,5},{38,6},{39,7},{40,8},{41... | collective-permute-start | bytes 1544 | tf_op jit(solution)/shard_map/ppermute | solution.py:537
  20.3 18.7 %collective-permute-start.62 = (f32[1,128]{1,0:T(1,128)S(1)}, f32[1,128]{1,0:T(1,128)S(1)}, u32[]{:S(2)}, u32[]{:S(2)}) collective-permute-start(f32[1,128]{1,0:T(1,128)S(1)} %add_add_fusion.19.refs_3_), channel_id=1, source_target_pairs={{16,0},{17,1},{18,2},{19,3},{20,4},{21,5},{22,6},{23,7},{24,8},{25... | collective-permute-start | bytes 1544 | tf_op jit(solution)/shard_map/ppermute | solution.py:537
  39.0 19.4 %collective-permute-start.67 = (f32[1,128]{1,0:T(1,128)S(1)}, f32[1,128]{1,0:T(1,128)S(1)}, u32[]{:S(2)}, u32[]{:S(2)}) collective-permute-start(f32[1,128]{1,0:T(1,128)S(1)} %add_add_fusion.18.refs_3_), channel_id=1, source_target_pairs={{192,0},{193,1},{194,2},{195,3},{196,4},{197,5},{198,6},{199,7},{2... | collective-permute-start | bytes 1544 | tf_op jit(solution)/shard_map/ppermute | solution.py:537
  43.6 14.8 %collective-permute-start.66 = (f32[1,128]{1,0:T(1,128)S(1)}, f32[1,128]{1,0:T(1,128)S(1)}, u32[]{:S(2)}, u32[]{:S(2)}) collective-permute-start(f32[1,128]{1,0:T(1,128)S(1)} %add_add_fusion.18.refs_3_), channel_id=1, source_target_pairs={{128,0},{129,1},{130,2},{131,3},{132,4},{133,5},{134,6},{135,7},{1... | collective-permute-start | bytes 1544 | tf_op jit(solution)/shard_map/ppermute | solution.py:537
  44.6 13.8 %collective-permute-start.65 = (f32[1,128]{1,0:T(1,128)S(1)}, f32[1,128]{1,0:T(1,128)S(1)}, u32[]{:S(2)}, u32[]{:S(2)}) collective-permute-start(f32[1,128]{1,0:T(1,128)S(1)} %add_add_fusion.18.refs_3_), channel_id=1, source_target_pairs={{64,0},{65,1},{66,2},{67,3},{68,4},{69,5},{70,6},{71,7},{72,8},{73... | collective-permute-start | bytes 1544 | tf_op jit(solution)/shard_map/ppermute | solution.py:537
  62.9 5.1 %collective-permute-start.69 = (f32[32,135]{1,0:T(8,128)S(1)}, f32[32,135]{1,0:T(8,128)S(1)}, u32[]{:S(2)}, u32[]{:S(2)}) collective-permute-start(f32[32,135]{1,0:T(8,128)S(1)} %pad_maximum_fusion.21), channel_id=1, source_target_pairs={{3,0},{2,1},{1,2},{0,3},{7,4},{6,5},{5,6},{4,7},{11,8},{10,9},{9,1... | collective-permute-start | bytes 51848 | tf_op jit(solution)/shard_map/ppermute | solution.py:524
  68.0 4.2 %collective-permute-start.70 = (f32[64,135]{1,0:T(8,128)S(1)}, f32[64,135]{1,0:T(8,128)S(1)}, u32[]{:S(2)}, u32[]{:S(2)}) collective-permute-start(f32[64,135]{1,0:T(8,128)S(1)} %constant_dynamic-update-slice_fusion.6.refs_1_), channel_id=1, source_target_pairs={{252,0},{0,4},{4,8},{8,12},{12,16},{16,20},{20,24},{24,28},{28,32}... | collective-permute-start | bytes 103688 | tf_op jit(solution)/shard_map/ppermute | solution.py:506
  82.1 5.1 %collective-permute-start.73 = (f32[32,135]{1,0:T(8,128)S(1)}, f32[32,135]{1,0:T(8,128)S(1)}, u32[]{:S(2)}, u32[]{:S(2)}) collective-permute-start(f32[32,135]{1,0:T(8,128)S(1)} %pad_maximum_fusion.22), channel_id=1, source_target_pairs={{3,0},{2,1},{1,2},{0,3},{7,4},{6,5},{5,6},{4,7},{11,8},{10,9},{9,1... | collective-permute-start | bytes 51848 | tf_op jit(solution)/shard_map/ppermute | solution.py:524
  87.3 11.3 %collective-permute-start.77 = (f32[64,135]{1,0:T(8,128)S(1)}, f32[64,135]{1,0:T(8,128)S(1)}, u32[]{:S(2)}, u32[]{:S(2)}) collective-permute-start(f32[64,135]{1,0:T(8,128)S(1)} %pad_maximum_fusion.6.refs_2_), channel_id=1, source_target_pairs={{8,0},{12,4},{16,8},{20,12},{24,16},{28,20},{32,24},{36,28},{40,32... | collective-permute-start | bytes 103688 | tf_op jit(solution)/shard_map/ppermute | solution.py:506
  87.9 10.7 %collective-permute-start.76 = (f32[64,135]{1,0:T(8,128)S(1)}, f32[64,135]{1,0:T(8,128)S(1)}, u32[]{:S(2)}, u32[]{:S(2)}) collective-permute-start(f32[64,135]{1,0:T(8,128)S(1)} %pad_maximum_fusion.6.refs_2_), channel_id=1, source_target_pairs={{4,0},{8,4},{12,8},{16,12},{20,16},{24,20},{28,24},{32,28},{36,32}... | collective-permute-start | bytes 103688 | tf_op jit(solution)/shard_map/ppermute | solution.py:506
  87.9 10.7 %collective-permute-start.75 = (f32[64,135]{1,0:T(8,128)S(1)}, f32[64,135]{1,0:T(8,128)S(1)}, u32[]{:S(2)}, u32[]{:S(2)}) collective-permute-start(f32[64,135]{1,0:T(8,128)S(1)} %pad_maximum_fusion.6.refs_2_), channel_id=1, source_target_pairs={{252,0},{0,4},{4,8},{8,12},{12,16},{16,20},{20,24},{24,28},{28,32}... | collective-permute-start | bytes 103688 | tf_op jit(solution)/shard_map/ppermute | solution.py:506
  88.4 10.2 %collective-permute-start.74 = (f32[64,135]{1,0:T(8,128)S(1)}, f32[64,135]{1,0:T(8,128)S(1)}, u32[]{:S(2)}, u32[]{:S(2)}) collective-permute-start(f32[64,135]{1,0:T(8,128)S(1)} %pad_maximum_fusion.6.refs_2_), channel_id=1, source_target_pairs={{248,0},{252,4},{0,8},{4,12},{8,16},{12,20},{16,24},{20,28},{24,32... | collective-permute-start | bytes 103688 | tf_op jit(solution)/shard_map/ppermute | solution.py:506
  100.3 3.8 collective-permute-start.78
  104.2 5.1 %collective-permute-start.79 = (f32[32,135]{1,0:T(8,128)S(1)}, f32[32,135]{1,0:T(8,128)S(1)}, u32[]{:S(2)}, u32[]{:S(2)}) collective-permute-start(f32[32,135]{1,0:T(8,128)S(1)} %pad_maximum_fusion.23), channel_id=1, source_target_pairs={{3,0},{2,1},{1,2},{0,3},{7,4},{6,5},{5,6},{4,7},{11,8},{10,9},{9,1... | collective-permute-start | bytes 51848 | tf_op jit(solution)/shard_map/ppermute | solution.py:524
  118.6 5.1 %collective-permute-start.83 = (f32[32,135]{1,0:T(8,128)S(1)}, f32[32,135]{1,0:T(8,128)S(1)}, u32[]{:S(2)}, u32[]{:S(2)}) collective-permute-start(f32[32,135]{1,0:T(8,128)S(1)} %pad_maximum_fusion.24), channel_id=1, source_target_pairs={{3,0},{2,1},{1,2},{0,3},{7,4},{6,5},{5,6},{4,7},{11,8},{10,9},{9,1... | collective-permute-start | bytes 51848 | tf_op jit(solution)/shard_map/ppermute | solution.py:524
  123.8 5.8 %collective-permute-start.87 = (f32[64,135]{1,0:T(8,128)S(1)}, f32[64,135]{1,0:T(8,128)S(1)}, u32[]{:S(2)}, u32[]{:S(2)}) collective-permute-start(f32[64,135]{1,0:T(8,128)S(1)} %pad_maximum_fusion.8.refs_2_), channel_id=1, source_target_pairs={{8,0},{12,4},{16,8},{20,12},{24,16},{28,20},{32,24},{36,28},{40,32... | collective-permute-start | bytes 103688 | tf_op jit(solution)/shard_map/ppermute | solution.py:506
  125.5 4.1 %collective-permute-start.86 = (f32[64,135]{1,0:T(8,128)S(1)}, f32[64,135]{1,0:T(8,128)S(1)}, u32[]{:S(2)}, u32[]{:S(2)}) collective-permute-start(f32[64,135]{1,0:T(8,128)S(1)} %pad_maximum_fusion.8.refs_2_), channel_id=1, source_target_pairs={{4,0},{8,4},{12,8},{16,12},{20,16},{24,20},{28,24},{32,28},{36,32}... | collective-permute-start | bytes 103688 | tf_op jit(solution)/shard_map/ppermute | solution.py:506
  125.5 6.6 %collective-permute-start.85 = (f32[64,135]{1,0:T(8,128)S(1)}, f32[64,135]{1,0:T(8,128)S(1)}, u32[]{:S(2)}, u32[]{:S(2)}) collective-permute-start(f32[64,135]{1,0:T(8,128)S(1)} %pad_maximum_fusion.8.refs_2_), channel_id=1, source_target_pairs={{252,0},{0,4},{4,8},{8,12},{12,16},{16,20},{20,24},{24,28},{28,32}... | collective-permute-start | bytes 103688 | tf_op jit(solution)/shard_map/ppermute | solution.py:506
  126.0 7.5 %collective-permute-start.84 = (f32[64,135]{1,0:T(8,128)S(1)}, f32[64,135]{1,0:T(8,128)S(1)}, u32[]{:S(2)}, u32[]{:S(2)}) collective-permute-start(f32[64,135]{1,0:T(8,128)S(1)} %pad_maximum_fusion.8.refs_2_), channel_id=1, source_target_pairs={{248,0},{252,4},{0,8},{4,12},{8,16},{12,20},{16,24},{20,28},{24,32... | collective-permute-start | bytes 103688 | tf_op jit(solution)/shard_map/ppermute | solution.py:506
  139.0 5.1 %collective-permute-start.89 = (f32[32,135]{1,0:T(8,128)S(1)}, f32[32,135]{1,0:T(8,128)S(1)}, u32[]{:S(2)}, u32[]{:S(2)}) collective-permute-start(f32[32,135]{1,0:T(8,128)S(1)} %pad_maximum_fusion.25), channel_id=1, source_target_pairs={{3,0},{2,1},{1,2},{0,3},{7,4},{6,5},{5,6},{4,7},{11,8},{10,9},{9,1... | collective-permute-start | bytes 51848 | tf_op jit(solution)/shard_map/ppermute | solution.py:524
  153.4 5.1 %collective-permute-start.93 = (f32[32,135]{1,0:T(8,128)S(1)}, f32[32,135]{1,0:T(8,128)S(1)}, u32[]{:S(2)}, u32[]{:S(2)}) collective-permute-start(f32[32,135]{1,0:T(8,128)S(1)} %pad_maximum_fusion.26), channel_id=1, source_target_pairs={{3,0},{2,1},{1,2},{0,3},{7,4},{6,5},{5,6},{4,7},{11,8},{10,9},{9,1... | collective-permute-start | bytes 51848 | tf_op jit(solution)/shard_map/ppermute | solution.py:524
  158.5 4.4 %collective-permute-start.97 = (f32[64,135]{1,0:T(8,128)S(1)}, f32[64,135]{1,0:T(8,128)S(1)}, u32[]{:S(2)}, u32[]{:S(2)}) collective-permute-start(f32[64,135]{1,0:T(8,128)S(1)} %pad_maximum_fusion.10.refs_2_), channel_id=1, source_target_pairs={{8,0},{12,4},{16,8},{20,12},{24,16},{28,20},{32,24},{36,28},{40,32... | collective-permute-start | bytes 103688 | tf_op jit(solution)/shard_map/ppermute | solution.py:506
  161.1 5.9 %collective-permute-start.95 = (f32[64,135]{1,0:T(8,128)S(1)}, f32[64,135]{1,0:T(8,128)S(1)}, u32[]{:S(2)}, u32[]{:S(2)}) collective-permute-start(f32[64,135]{1,0:T(8,128)S(1)} %pad_maximum_fusion.10.refs_2_), channel_id=1, source_target_pairs={{252,0},{0,4},{4,8},{8,12},{12,16},{16,20},{20,24},{24,28},{28,32}... | collective-permute-start | bytes 103688 | tf_op jit(solution)/shard_map/ppermute | solution.py:506
  161.6 6.7 %collective-permute-start.94 = (f32[64,135]{1,0:T(8,128)S(1)}, f32[64,135]{1,0:T(8,128)S(1)}, u32[]{:S(2)}, u32[]{:S(2)}) collective-permute-start(f32[64,135]{1,0:T(8,128)S(1)} %pad_maximum_fusion.10.refs_2_), channel_id=1, source_target_pairs={{248,0},{252,4},{0,8},{4,12},{8,16},{12,20},{16,24},{20,28},{24,32... | collective-permute-start | bytes 103688 | tf_op jit(solution)/shard_map/ppermute | solution.py:506
  173.8 5.1 %collective-permute-start.99 = (f32[32,135]{1,0:T(8,128)S(1)}, f32[32,135]{1,0:T(8,128)S(1)}, u32[]{:S(2)}, u32[]{:S(2)}) collective-permute-start(f32[32,135]{1,0:T(8,128)S(1)} %pad_maximum_fusion.27), channel_id=1, source_target_pairs={{3,0},{2,1},{1,2},{0,3},{7,4},{6,5},{5,6},{4,7},{11,8},{10,9},{9,1... | collective-permute-start | bytes 51848 | tf_op jit(solution)/shard_map/ppermute | solution.py:524
  188.3 5.5 %collective-permute-start.103 = (f32[32,135]{1,0:T(8,128)S(1)}, f32[32,135]{1,0:T(8,128)S(1)}, u32[]{:S(2)}, u32[]{:S(2)}) collective-permute-start(f32[32,135]{1,0:T(8,128)S(1)} %pad_maximum_fusion.28), channel_id=1, source_target_pairs={{3,0},{2,1},{1,2},{0,3},{7,4},{6,5},{5,6},{4,7},{11,8},{10,9},{9,1... | collective-permute-start | bytes 51848 | tf_op jit(solution)/shard_map/ppermute | solution.py:524
  193.8 4.3 %collective-permute-start.107 = (f32[64,135]{1,0:T(8,128)S(1)}, f32[64,135]{1,0:T(8,128)S(1)}, u32[]{:S(2)}, u32[]{:S(2)}) collective-permute-start(f32[64,135]{1,0:T(8,128)S(1)} %pad_maximum_fusion.12.refs_2_), channel_id=1, source_target_pairs={{8,0},{12,4},{16,8},{20,12},{24,16},{28,20},{32,24},{36,28},{40,32... | collective-permute-start | bytes 103688 | tf_op jit(solution)/shard_map/ppermute | solution.py:506
  195.9 5.9 %collective-permute-start.105 = (f32[64,135]{1,0:T(8,128)S(1)}, f32[64,135]{1,0:T(8,128)S(1)}, u32[]{:S(2)}, u32[]{:S(2)}) collective-permute-start(f32[64,135]{1,0:T(8,128)S(1)} %pad_maximum_fusion.12.refs_2_), channel_id=1, source_target_pairs={{252,0},{0,4},{4,8},{8,12},{12,16},{16,20},{20,24},{24,28},{28,32}... | collective-permute-start | bytes 103688 | tf_op jit(solution)/shard_map/ppermute | solution.py:506
  196.4 6.7 %collective-permute-start.104 = (f32[64,135]{1,0:T(8,128)S(1)}, f32[64,135]{1,0:T(8,128)S(1)}, u32[]{:S(2)}, u32[]{:S(2)}) collective-permute-start(f32[64,135]{1,0:T(8,128)S(1)} %pad_maximum_fusion.12.refs_2_), channel_id=1, source_target_pairs={{248,0},{252,4},{0,8},{4,12},{8,16},{12,20},{16,24},{20,28},{24,32... | collective-permute-start | bytes 103688 | tf_op jit(solution)/shard_map/ppermute | solution.py:506
  208.7 5.1 %collective-permute-start.109 = (f32[32,135]{1,0:T(8,128)S(1)}, f32[32,135]{1,0:T(8,128)S(1)}, u32[]{:S(2)}, u32[]{:S(2)}) collective-permute-start(f32[32,135]{1,0:T(8,128)S(1)} %pad_maximum_fusion.29), channel_id=1, source_target_pairs={{3,0},{2,1},{1,2},{0,3},{7,4},{6,5},{5,6},{4,7},{11,8},{10,9},{9,1... | collective-permute-start | bytes 51848 | tf_op jit(solution)/shard_map/ppermute | solution.py:524
  223.1 5.1 %collective-permute-start.113 = (f32[32,135]{1,0:T(8,128)S(1)}, f32[32,135]{1,0:T(8,128)S(1)}, u32[]{:S(2)}, u32[]{:S(2)}) collective-permute-start(f32[32,135]{1,0:T(8,128)S(1)} %pad_maximum_fusion.30), channel_id=1, source_target_pairs={{3,0},{2,1},{1,2},{0,3},{7,4},{6,5},{5,6},{4,7},{11,8},{10,9},{9,1... | collective-permute-start | bytes 51848 | tf_op jit(solution)/shard_map/ppermute | solution.py:524
  228.2 4.3 %collective-permute-start.117 = (f32[64,135]{1,0:T(8,128)S(1)}, f32[64,135]{1,0:T(8,128)S(1)}, u32[]{:S(2)}, u32[]{:S(2)}) collective-permute-start(f32[64,135]{1,0:T(8,128)S(1)} %pad_maximum_fusion.14.refs_2_), channel_id=1, source_target_pairs={{8,0},{12,4},{16,8},{20,12},{24,16},{28,20},{32,24},{36,28},{40,32... | collective-permute-start | bytes 103688 | tf_op jit(solution)/shard_map/ppermute | solution.py:506
  230.3 5.9 %collective-permute-start.115 = (f32[64,135]{1,0:T(8,128)S(1)}, f32[64,135]{1,0:T(8,128)S(1)}, u32[]{:S(2)}, u32[]{:S(2)}) collective-permute-start(f32[64,135]{1,0:T(8,128)S(1)} %pad_maximum_fusion.14.refs_2_), channel_id=1, source_target_pairs={{252,0},{0,4},{4,8},{8,12},{12,16},{16,20},{20,24},{24,28},{28,32}... | collective-permute-start | bytes 103688 | tf_op jit(solution)/shard_map/ppermute | solution.py:506
  230.8 6.7 %collective-permute-start.114 = (f32[64,135]{1,0:T(8,128)S(1)}, f32[64,135]{1,0:T(8,128)S(1)}, u32[]{:S(2)}, u32[]{:S(2)}) collective-permute-start(f32[64,135]{1,0:T(8,128)S(1)} %pad_maximum_fusion.14.refs_2_), channel_id=1, source_target_pairs={{248,0},{252,4},{0,8},{4,12},{8,16},{12,20},{16,24},{20,28},{24,32... | collective-permute-start | bytes 103688 | tf_op jit(solution)/shard_map/ppermute | solution.py:506
  239.2 3.8 collective-permute-start.118
  243.1 5.3 %collective-permute-start.119 = (f32[32,135]{1,0:T(8,128)S(1)}, f32[32,135]{1,0:T(8,128)S(1)}, u32[]{:S(2)}, u32[]{:S(2)}) collective-permute-start(f32[32,135]{1,0:T(8,128)S(1)} %pad_maximum_fusion.31), channel_id=1, source_target_pairs={{3,0},{2,1},{1,2},{0,3},{7,4},{6,5},{5,6},{4,7},{11,8},{10,9},{9,1... | collective-permute-start | bytes 51848 | tf_op jit(solution)/shard_map/ppermute | solution.py:524
  257.7 5.1 %collective-permute-start.123 = (f32[32,135]{1,0:T(8,128)S(1)}, f32[32,135]{1,0:T(8,128)S(1)}, u32[]{:S(2)}, u32[]{:S(2)}) collective-permute-start(f32[32,135]{1,0:T(8,128)S(1)} %pad_maximum_fusion.32), channel_id=1, source_target_pairs={{3,0},{2,1},{1,2},{0,3},{7,4},{6,5},{5,6},{4,7},{11,8},{10,9},{9,1... | collective-permute-start | bytes 51848 | tf_op jit(solution)/shard_map/ppermute | solution.py:524
  262.8 4.3 %collective-permute-start.127 = (f32[64,135]{1,0:T(8,128)S(1)}, f32[64,135]{1,0:T(8,128)S(1)}, u32[]{:S(2)}, u32[]{:S(2)}) collective-permute-start(f32[64,135]{1,0:T(8,128)S(1)} %pad_maximum_fusion.16.refs_2_), channel_id=1, source_target_pairs={{8,0},{12,4},{16,8},{20,12},{24,16},{28,20},{32,24},{36,28},{40,32... | collective-permute-start | bytes 103688 | tf_op jit(solution)/shard_map/ppermute | solution.py:506
  264.9 5.9 %collective-permute-start.125 = (f32[64,135]{1,0:T(8,128)S(1)}, f32[64,135]{1,0:T(8,128)S(1)}, u32[]{:S(2)}, u32[]{:S(2)}) collective-permute-start(f32[64,135]{1,0:T(8,128)S(1)} %pad_maximum_fusion.16.refs_2_), channel_id=1, source_target_pairs={{252,0},{0,4},{4,8},{8,12},{12,16},{16,20},{20,24},{24,28},{28,32}... | collective-permute-start | bytes 103688 | tf_op jit(solution)/shard_map/ppermute | solution.py:506
  265.4 6.7 %collective-permute-start.124 = (f32[64,135]{1,0:T(8,128)S(1)}, f32[64,135]{1,0:T(8,128)S(1)}, u32[]{:S(2)}, u32[]{:S(2)}) collective-permute-start(f32[64,135]{1,0:T(8,128)S(1)} %pad_maximum_fusion.16.refs_2_), channel_id=1, source_target_pairs={{248,0},{252,4},{0,8},{4,12},{8,16},{12,20},{16,24},{20,28},{24,32... | collective-permute-start | bytes 103688 | tf_op jit(solution)/shard_map/ppermute | solution.py:506
  277.7 5.1 %collective-permute-start.129 = (f32[32,135]{1,0:T(8,128)S(1)}, f32[32,135]{1,0:T(8,128)S(1)}, u32[]{:S(2)}, u32[]{:S(2)}) collective-permute-start(f32[32,135]{1,0:T(8,128)S(1)} %pad_maximum_fusion.33), channel_id=1, source_target_pairs={{3,0},{2,1},{1,2},{0,3},{7,4},{6,5},{5,6},{4,7},{11,8},{10,9},{9,1... | collective-permute-start | bytes 51848 | tf_op jit(solution)/shard_map/ppermute | solution.py:524
  292.1 5.1 %collective-permute-start.133 = (f32[32,135]{1,0:T(8,128)S(1)}, f32[32,135]{1,0:T(8,128)S(1)}, u32[]{:S(2)}, u32[]{:S(2)}) collective-permute-start(f32[32,135]{1,0:T(8,128)S(1)} %pad_maximum_fusion.34), channel_id=1, source_target_pairs={{3,0},{2,1},{1,2},{0,3},{7,4},{6,5},{5,6},{4,7},{11,8},{10,9},{9,1... | collective-permute-start | bytes 51848 | tf_op jit(solution)/shard_map/ppermute | solution.py:524
  297.3 5.7 %collective-permute-start.137 = (f32[64,135]{1,0:T(8,128)S(1)}, f32[64,135]{1,0:T(8,128)S(1)}, u32[]{:S(2)}, u32[]{:S(2)}) collective-permute-start(f32[64,135]{1,0:T(8,128)S(1)} %pad_maximum_fusion.18.refs_2_), channel_id=1, source_target_pairs={{8,0},{12,4},{16,8},{20,12},{24,16},{28,20},{32,24},{36,28},{40,32... | collective-permute-start | bytes 103688 | tf_op jit(solution)/shard_map/ppermute | solution.py:506
  301.3 5.9 %collective-permute-start.135 = (f32[64,135]{1,0:T(8,128)S(1)}, f32[64,135]{1,0:T(8,128)S(1)}, u32[]{:S(2)}, u32[]{:S(2)}) collective-permute-start(f32[64,135]{1,0:T(8,128)S(1)} %pad_maximum_fusion.18.refs_2_), channel_id=1, source_target_pairs={{252,0},{0,4},{4,8},{8,12},{12,16},{16,20},{20,24},{24,28},{28,32}... | collective-permute-start | bytes 103688 | tf_op jit(solution)/shard_map/ppermute | solution.py:506
  301.8 6.7 %collective-permute-start.134 = (f32[64,135]{1,0:T(8,128)S(1)}, f32[64,135]{1,0:T(8,128)S(1)}, u32[]{:S(2)}, u32[]{:S(2)}) collective-permute-start(f32[64,135]{1,0:T(8,128)S(1)} %pad_maximum_fusion.18.refs_2_), channel_id=1, source_target_pairs={{248,0},{252,4},{0,8},{4,12},{8,16},{12,20},{16,24},{20,28},{24,32... | collective-permute-start | bytes 103688 | tf_op jit(solution)/shard_map/ppermute | solution.py:506
  314.0 5.1 %collective-permute-start.139 = (f32[32,135]{1,0:T(8,128)S(1)}, f32[32,135]{1,0:T(8,128)S(1)}, u32[]{:S(2)}, u32[]{:S(2)}) collective-permute-start(f32[32,135]{1,0:T(8,128)S(1)} %pad_maximum_fusion.35), channel_id=1, source_target_pairs={{3,0},{2,1},{1,2},{0,3},{7,4},{6,5},{5,6},{4,7},{11,8},{10,9},{9,1... | collective-permute-start | bytes 51848 | tf_op jit(solution)/shard_map/ppermute | solution.py:524
  319.3 4.4 %collective-permute-start.140 = (f32[64,135]{1,0:T(8,128)S(1)}, f32[64,135]{1,0:T(8,128)S(1)}, u32[]{:S(2)}, u32[]{:S(2)}) collective-permute-start(f32[64,135]{1,0:T(8,128)S(1)} %pad_maximum_fusion.19.refs_1_), channel_id=1, source_target_pairs={{252,0},{0,4},{4,8},{8,12},{12,16},{16,20},{20,24},{24,28},{28,32}... | collective-permute-start | bytes 103688 | tf_op jit(solution)/shard_map/ppermute | solution.py:506
  329.1 5.1 %collective-permute-start.143 = (f32[32,135]{1,0:T(8,128)S(1)}, f32[32,135]{1,0:T(8,128)S(1)}, u32[]{:S(2)}, u32[]{:S(2)}) collective-permute-start(f32[32,135]{1,0:T(8,128)S(1)} %pad_maximum_fusion.36), channel_id=1, source_target_pairs={{3,0},{2,1},{1,2},{0,3},{7,4},{6,5},{5,6},{4,7},{11,8},{10,9},{9,1... | collective-permute-start | bytes 51848 | tf_op jit(solution)/shard_map/ppermute | solution.py:524
  334.3 5.9 %collective-permute-start.147 = (f32[64,135]{1,0:T(8,128)S(1)}, f32[64,135]{1,0:T(8,128)S(1)}, u32[]{:S(2)}, u32[]{:S(2)}) collective-permute-start(f32[64,135]{1,0:T(8,128)S(1)} %pad_maximum_fusion.20.refs_2_), channel_id=1, source_target_pairs={{8,0},{12,4},{16,8},{20,12},{24,16},{28,20},{32,24},{36,28},{40,32... | collective-permute-start | bytes 103688 | tf_op jit(solution)/shard_map/ppermute | solution.py:506
  338.2 5.9 %collective-permute-start.145 = (f32[64,135]{1,0:T(8,128)S(1)}, f32[64,135]{1,0:T(8,128)S(1)}, u32[]{:S(2)}, u32[]{:S(2)}) collective-permute-start(f32[64,135]{1,0:T(8,128)S(1)} %pad_maximum_fusion.20.refs_2_), channel_id=1, source_target_pairs={{252,0},{0,4},{4,8},{8,12},{12,16},{16,20},{20,24},{24,28},{28,32}... | collective-permute-start | bytes 103688 | tf_op jit(solution)/shard_map/ppermute | solution.py:506
  338.7 6.7 %collective-permute-start.144 = (f32[64,135]{1,0:T(8,128)S(1)}, f32[64,135]{1,0:T(8,128)S(1)}, u32[]{:S(2)}, u32[]{:S(2)}) collective-permute-start(f32[64,135]{1,0:T(8,128)S(1)} %pad_maximum_fusion.20.refs_2_), channel_id=1, source_target_pairs={{248,0},{252,4},{0,8},{4,12},{8,16},{12,20},{16,24},{20,28},{24,32... | collective-permute-start | bytes 103688 | tf_op jit(solution)/shard_map/ppermute | solution.py:506
  347.3 4.9 %collective-permute-start.150 = (f32[16,128]{1,0:T(8,128)S(1)}, f32[16,128]{1,0:T(8,128)S(1)}, u32[]{:S(2)}, u32[]{:S(2)}) collective-permute-start(f32[16,128]{1,0:T(8,128)S(1)} %get-tuple-element.198), channel_id=1, source_target_pairs={{3,0},{2,1},{1,2},{0,3},{7,4},{6,5},{5,6},{4,7},{11,8},{10,9},{9,1... | collective-permute-start | bytes 24584 | tf_op jit(solution)/shard_map/ppermute | solution.py:537
  350.3 5.2 %collective-permute-start.149 = (f32[16,128]{1,0:T(8,128)S(1)}, f32[16,128]{1,0:T(8,128)S(1)}, u32[]{:S(2)}, u32[]{:S(2)}) collective-permute-start(f32[16,128]{1,0:T(8,128)S(1)} %get-tuple-element.198), channel_id=1, source_target_pairs={{2,0},{3,1},{0,2},{1,3},{6,4},{7,5},{4,6},{5,7},{10,8},{11,9},{8,1... | collective-permute-start | bytes 24584 | tf_op jit(solution)/shard_map/ppermute | solution.py:537
  350.3 5.2 %collective-permute-start.148 = (f32[16,128]{1,0:T(8,128)S(1)}, f32[16,128]{1,0:T(8,128)S(1)}, u32[]{:S(2)}, u32[]{:S(2)}) collective-permute-start(f32[16,128]{1,0:T(8,128)S(1)} %get-tuple-element.198), channel_id=1, source_target_pairs={{1,0},{0,1},{3,2},{2,3},{5,4},{4,5},{7,6},{6,7},{9,8},{8,9},{11,10... | collective-permute-start | bytes 24584 | tf_op jit(solution)/shard_map/ppermute | solution.py:537
  359.8 19.3 %collective-permute-start.156 = (f32[16,128]{1,0:T(8,128)S(1)}, f32[16,128]{1,0:T(8,128)S(1)}, u32[]{:S(2)}, u32[]{:S(2)}) collective-permute-start(f32[16,128]{1,0:T(8,128)S(1)} %add_add_fusion.14), channel_id=1, source_target_pairs={{48,0},{49,1},{50,2},{51,3},{52,4},{53,5},{54,6},{55,7},{56,8},{57... | collective-permute-start | bytes 24584 | tf_op jit(solution)/shard_map/ppermute | solution.py:537
  368.0 11.0 %collective-permute-start.155 = (f32[16,128]{1,0:T(8,128)S(1)}, f32[16,128]{1,0:T(8,128)S(1)}, u32[]{:S(2)}, u32[]{:S(2)}) collective-permute-start(f32[16,128]{1,0:T(8,128)S(1)} %add_add_fusion.14), channel_id=1, source_target_pairs={{32,0},{33,1},{34,2},{35,3},{36,4},{37,5},{38,6},{39,7},{40,8},{41... | collective-permute-start | bytes 24584 | tf_op jit(solution)/shard_map/ppermute | solution.py:537
  376.2 5.2 %collective-permute-start.154 = (f32[16,128]{1,0:T(8,128)S(1)}, f32[16,128]{1,0:T(8,128)S(1)}, u32[]{:S(2)}, u32[]{:S(2)}) collective-permute-start(f32[16,128]{1,0:T(8,128)S(1)} %add_add_fusion.14), channel_id=1, source_target_pairs={{16,0},{17,1},{18,2},{19,3},{20,4},{21,5},{22,6},{23,7},{24,8},{25... | collective-permute-start | bytes 24584 | tf_op jit(solution)/shard_map/ppermute | solution.py:537
  381.3 9.5 %collective-permute-start.159 = (f32[16,128]{1,0:T(8,128)S(1)}, f32[16,128]{1,0:T(8,128)S(1)}, u32[]{:S(2)}, u32[]{:S(2)}) collective-permute-start(f32[16,128]{1,0:T(8,128)S(1)} %add_add_fusion.13), channel_id=1, source_target_pairs={{192,0},{193,1},{194,2},{195,3},{196,4},{197,5},{198,6},{199,7},{2... | collective-permute-start | bytes 24584 | tf_op jit(solution)/shard_map/ppermute | solution.py:537
  388.4 7.6 %collective-permute-start.158 = (f32[16,128]{1,0:T(8,128)S(1)}, f32[16,128]{1,0:T(8,128)S(1)}, u32[]{:S(2)}, u32[]{:S(2)}) collective-permute-start(f32[16,128]{1,0:T(8,128)S(1)} %add_add_fusion.13), channel_id=1, source_target_pairs={{128,0},{129,1},{130,2},{131,3},{132,4},{133,5},{134,6},{135,7},{1... | collective-permute-start | bytes 24584 | tf_op jit(solution)/shard_map/ppermute | solution.py:537
  390.3 5.7 %collective-permute-start.157 = (f32[16,128]{1,0:T(8,128)S(1)}, f32[16,128]{1,0:T(8,128)S(1)}, u32[]{:S(2)}, u32[]{:S(2)}) collective-permute-start(f32[16,128]{1,0:T(8,128)S(1)} %add_add_fusion.13), channel_id=1, source_target_pairs={{64,0},{65,1},{66,2},{67,3},{68,4},{69,5},{70,6},{71,7},{72,8},{73... | collective-permute-start | bytes 24584 | tf_op jit(solution)/shard_map/ppermute | solution.py:537
  (59 other events, 363.6 us)
